TPU v7x, 32 devices: a whole 2x2x4 slice. The times are simulated.
32 devices in a mesh: energy: 8 (over z, y), rows: 4 (over x, core).
Axes of the slice: x: 2, y: 2, z: 4, core: 2. Of those that a mesh axis runs over, the one named last changes fastest.
Arguments:
- green_window: bfloat16 [2, 2, 16, 4, 9216], P(None, None, 'energy', 'rows'), may hold values from -6 to 6
- screened: bfloat16 [2, 2, 16, 4, 9216], P(None, None, None, 'rows', 'energy'), may hold values from -6 to 6
- retarded: bfloat16 [2, 16, 4, 3, 96, 192], P(None, 'energy', 'rows'), may hold values from -0.375 to 0.375
- energy_order: int32 [16], replicated, may hold values from 0 to 15, each once
- window_start: int32 [4], P('rows'), may hold values from 0 to 96
Outputs:
- density: float32 [2, 2, 16, 4, 192], P(None, None, 'energy', 'rows')
Inputs may be any that keep to these rules, and one draw needn't show every extreme that they name: A permutation of the energy indices: slot s holds energy energy_order[s]. Block row i's window covers its orbitals window_start[i] to window_start[i] + 95.
All inputs are finite; a program needn't handle non-finite values.
Results may differ from a plain program's by a relative error of at most 0.0029.
Values may be sent and summed in bfloat16 or wider, within the bound.
No kernel may reach another device: no remote copies, remote signals or barrier semaphores. Data moves between devices by JAX's collectives and lax.ppermute only.
A program may use at most 64 MiB of HBM per device.

v0:
```python
import math

import jax
import jax.numpy as jnp
from jax import lax
from jax.sharding import PartitionSpec as P


def with_halo(cells, sides, width):
    for axis, dim in sides:
        count = lax.axis_size(axis)
        ends = count - 1
        head = lax.slice_in_dim(cells, 0, width, axis=dim)
        tail = lax.slice_in_dim(cells, cells.shape[dim] - width, cells.shape[dim], axis=dim)
        cells = jnp.concatenate(
            [
                lax.ppermute(tail, axis, [(i, (i + 1) % count) for i in range(ends)]),
                cells,
                lax.ppermute(head, axis, [((i + 1) % count, i) for i in range(ends)]),
            ],
            axis=dim,
        )
    return cells


def phase_table(count_rows, count_cols, modulus, direction):
    left = lax.broadcasted_iota(jnp.int32, (count_rows, count_cols), 0)
    right = lax.broadcasted_iota(jnp.int32, (count_rows, count_cols), 1)
    turns = left * right % modulus
    angle = direction * 2.0 * math.pi / modulus * turns.astype(jnp.float32)
    return (jnp.cos(angle), jnp.sin(angle))


def complex_einsum(form, left_re, left_im, right_re, right_im):
    highest = lax.Precision.HIGHEST
    real_part = jnp.einsum(form, left_re, right_re, precision=highest) - jnp.einsum(
        form, left_im, right_im, precision=highest
    )
    imag_part = jnp.einsum(form, left_re, right_im, precision=highest) + jnp.einsum(
        form, left_im, right_re, precision=highest
    )
    return (real_part, imag_part)


def transform(data_re, data_im, inner_count, direction):
    total = data_re.shape[0]
    columns = data_re.shape[1]
    outer_count = total // inner_count
    shaped_re = data_re.reshape(inner_count, outer_count, columns)
    shaped_im = data_im.reshape(inner_count, outer_count, columns)
    first_re, first_im = phase_table(inner_count, inner_count, inner_count, direction)
    section_re, section_im = complex_einsum("kb,bac->kac", first_re, first_im, shaped_re, shaped_im)
    twist_re, twist_im = phase_table(inner_count, outer_count, total, direction)
    turned_re = section_re * twist_re[:, :, None] - section_im * twist_im[:, :, None]
    turned_im = section_re * twist_im[:, :, None] + section_im * twist_re[:, :, None]
    second_re, second_im = phase_table(outer_count, outer_count, outer_count, direction)
    final_re, final_im = complex_einsum("kac,am->mkc", turned_re, turned_im, second_re, second_im)
    return (final_re.reshape(total, columns), final_im.reshape(total, columns))


def window_product(part, right):
    return jnp.einsum("gepq,epa->geqa", part, right, preferred_element_type=jnp.float32)


def shards(green_window, screened, retarded, energy_order, window_start):
    per_device = green_window.shape[2]
    slab = retarded.shape[4]
    width = retarded.shape[5]
    local = green_window[:, :, :, 0, :]
    spread = lax.all_to_all(local, "energy", split_axis=3, concat_axis=2, tiled=True)
    total = spread.shape[2]
    columns = spread.shape[3]
    inverse = jnp.argsort(energy_order)
    ordered = jnp.take(spread, inverse, axis=2)
    green_cols = (
        jnp.transpose(ordered, (1, 2, 0, 3)).reshape(2, total, 2 * columns).astype(jnp.float32)
    )
    screen_local = screened[:, :, :, 0, :]
    screen_cols = (
        jnp.transpose(screen_local, (1, 2, 0, 3)).reshape(2, total, 2 * columns).astype(jnp.float32)
    )
    times_re, times_im = transform(green_cols[0], green_cols[1], per_device, -1.0)
    mixed_re = times_re * screen_cols[0] - times_im * screen_cols[1]
    mixed_im = times_re * screen_cols[1] + times_im * screen_cols[0]
    back_re, back_im = transform(mixed_re, mixed_im, per_device, 1.0)
    scale = 1.0 / total
    sigma_cols = jnp.stack([-back_im * scale, back_re * scale]).astype(jnp.bfloat16)
    sigma_slots = jnp.take(sigma_cols, energy_order, axis=1)
    sigma = jnp.transpose(sigma_slots.reshape(2, total, 2, columns), (2, 0, 1, 3))
    returned = lax.all_to_all(sigma, "energy", split_axis=2, concat_axis=3, tiled=True)
    bordered = with_halo(returned[:, :, :, None, :], (("rows", 3),), 1)
    sigma_all = bordered.reshape(2, 2, per_device, 3, slab, slab)
    dens_re = jnp.zeros((2, per_device, width), jnp.float32)
    dens_im = jnp.zeros((2, per_device, width), jnp.float32)
    for neighbour in range(3):
        part_re = sigma_all[:, 0, :, neighbour]
        part_im = sigma_all[:, 1, :, neighbour]
        right_re = retarded[0, :, 0, neighbour]
        right_im = retarded[1, :, 0, neighbour]
        inner_re = window_product(part_re, right_re) - window_product(part_im, right_im)
        inner_im = window_product(part_re, right_im) + window_product(part_im, right_re)
        wide_re = right_re.astype(jnp.float32)[None]
        wide_im = right_im.astype(jnp.float32)[None]
        dens_re = dens_re + jnp.sum(inner_re * wide_re + inner_im * wide_im, axis=2)
        dens_im = dens_im + jnp.sum(inner_im * wide_re - inner_re * wide_im, axis=2)
    own = sigma_all[:, :, :, 1].astype(jnp.float32)
    diagonal_part = jnp.diagonal(own, axis1=3, axis2=4)
    start = window_start[0]
    column_ids = lax.broadcasted_iota(jnp.int32, (slab, width), 1)
    window_ids = lax.broadcasted_iota(jnp.int32, (slab, width), 0)
    place = (column_ids == window_ids + start).astype(jnp.float32)
    direct = jnp.einsum("gcep,pa->gcea", diagonal_part, place, precision=lax.Precision.HIGHEST)
    density = jnp.stack([dens_re, dens_im], axis=1) + direct
    return density[:, :, :, None, :]


def solution(mesh):
    in_specs = (
        P(None, None, "energy", "rows", None),
        P(None, None, None, "rows", "energy"),
        P(None, "energy", "rows", None, None, None),
        P(),
        P("rows"),
    )
    out_specs = P(None, None, "energy", "rows", None)
    return jax.shard_map(shards, mesh=mesh, in_specs=in_specs, out_specs=out_specs, check_vma=False)
```

profile of v0, /device:TPU:1, one launch (start us, length us, event | category | flops | bytes accessed | tf_op | source)
XLA Modules:
  0.0 154.2 jit_solution(11007012804985680704)
XLA Ops:
  0.0 17.9 %copy.105 = bf16[2,2,2,1,9216]{2,1,0,4,3:T(2,128)(2,1)} copy(bf16[2,2,2,1,9216]{4,2,3,1,0:T(2,128)(2,1)} %param.5) | data formatting | bytes 294912 | tf_op args[0]
  17.9 8.8 %bitcast_bitcast_fusion = bf16[9216,2,2,2]{3,2,1,0:T(2,128)(2,1)} fusion(bf16[2,2,2,1,9216]{2,1,0,4,3:T(2,128)(2,1)} %copy.105), kind=kLoop, calls=%fused_computation.259 | loop fusion | bytes 294912
  26.8 15.2 %reshape.231 = bf16[8,2,4608]{2,1,0:T(2,128)(2,1)} reshape(bf16[9216,2,2,2]{3,2,1,0:T(2,128)(2,1)} %bitcast_bitcast_fusion) | data formatting | bytes 294912
  42.0 6.4 %all-to-all-start = ((bf16[8,2,4608]{2,1,0:T(2,128)(2,1)}), bf16[8,2,4608]{2,1,0:T(2,128)(2,1)S(1)}, u32[]{:S(2)}, u32[]{:S(2)}) async-start(bf16[8,2,4608]{2,1,0:T(2,128)(2,1)} %reshape.231), calls=%async_computation | async-start | bytes 294912 | tf_op jit(solution)/shard_map/all_to_all | solution.py:70
  48.4 1.2 sort.17
  50.0 0.1 squeeze.55
  50.2 0.1 squeeze.56
  51.0 3.7 %all-to-all-done = bf16[8,2,4608]{2,1,0:T(2,128)(2,1)S(1)} async-done(((bf16[8,2,4608]{2,1,0:T(2,128)(2,1)}), bf16[8,2,4608]{2,1,0:T(2,128)(2,1)S(1)}, u32[]{:S(2)}, u32[]{:S(2)}) %all-to-all-start) | async-done | bytes 147488 | tf_op jit(solution)/shard_map/all_to_all | solution.py:70
  54.7 21.4 %reshape.232 = bf16[9216,2,2,2]{3,2,1,0:T(2,128)(2,1)} reshape(bf16[8,2,4608]{2,1,0:T(2,128)(2,1)S(1)} %all-to-all-done) | data formatting | bytes 294912
  76.1 19.9 %copy.106 = bf16[2,2,2,8,1152]{4,1,2,3,0:T(2,128)(2,1)S(1)} copy(bf16[2,2,2,8,1152]{2,1,0,4,3:T(2,128)(2,1)} %bitcast.218) | data formatting | bytes 294912 | tf_op jit(solution)/shard_map/all_to_all | solution.py:70
  96.1 0.9 gather_fusion
  97.0 0.2 fusion.7
  97.2 0.8 slice_reduce_fusion.1
  98.0 0.4 fusion.76
  98.5 0.4 fusion.72
  98.9 0.4 convolution_subtract_fusion.3
  99.4 0.5 multiply_add_fusion.2
  99.9 0.3 fusion.18
  100.2 0.3 fusion.16
  100.6 0.3 convolution_subtract_fusion.2
  101.0 0.1 reshape.187
  101.1 0.3 convolution_add_fusion.2
  101.5 0.1 reshape.188
  101.7 0.7 fusion.24
  102.3 0.7 fusion.20
  103.0 0.7 convolution_subtract_fusion.1
  103.7 0.8 multiply_add_fusion
  104.5 0.3 fusion.12
  104.8 0.3 fusion.10
  105.1 0.3 fusion.3
  105.6 0.3 fusion.4
  106.0 0.3 pad_maximum_fusion
  106.4 0.9 gather_fusion.1
  107.2 0.9 fusion.6
  108.1 3.6 %all-to-all-start.1 = ((bf16[2,2,16,1152]{3,1,0,2:T(2,128)(2,1)}), bf16[2,2,16,1152]{3,1,0,2:T(2,128)(2,1)S(1)}, u32[]{:S(2)}, u32[]{:S(2)}) async-start(bf16[2,2,16,1152]{3,1,0,2:T(2,128)(2,1)} %fusion.6), calls=%async_computation.1 | async-start | bytes 294912 | tf_op jit(solution)/shard_map/all_to_all | solution.py:90
  111.7 0.1 bitcast_convert_fusion.5
  111.8 6.0 %all-to-all-done.1 = bf16[2,2,16,1152]{3,1,0,2:T(2,128)(2,1)S(1)} async-done(((bf16[2,2,16,1152]{3,1,0,2:T(2,128)(2,1)}), bf16[2,2,16,1152]{3,1,0,2:T(2,128)(2,1)S(1)}, u32[]{:S(2)}, u32[]{:S(2)}) %all-to-all-start.1) | async-done | bytes 147488 | tf_op jit(solution)/shard_map/all_to_all | solution.py:90
  117.9 0.2 concatenate.13
  118.1 0.1 copy.173
  118.2 0.2 fusion.36
  118.4 0.2 fusion.32
  118.6 6.1 %collective-permute-start = (bf16[2,2,2,1,9216]{4,2,1,0,3:T(2,128)(2,1)S(1)}, bf16[2,2,2,1,9216]{4,2,1,0,3:T(2,128)(2,1)}, u32[]{:S(2)}, u32[]{:S(2)}) collective-permute-start(bf16[2,2,2,1,9216]{4,2,1,0,3:T(2,128)(2,1)S(1)} %broadcast_in_dim.54), channel_id=1, source_target_pairs={{0,1},{1,2},{2,3},{4,5},{5,6},{6,7},{8,9},{9,10},{10,11},{12,13},{... | collective-permute-start | bytes 442376 | tf_op jit(solution)/shard_map/ppermute | solution.py:17
  124.8 1.9 %collective-permute-start.1 = (bf16[2,2,2,1,9216]{4,2,1,0,3:T(2,128)(2,1)S(1)}, bf16[2,2,2,1,9216]{4,2,1,0,3:T(2,128)(2,1)S(1)}, u32[]{:S(2)}, u32[]{:S(2)}) collective-permute-start(bf16[2,2,2,1,9216]{4,2,1,0,3:T(2,128)(2,1)S(1)} %broadcast_in_dim.54), channel_id=1, source_target_pairs={{1,0},{2,1},{3,2},{5,4},{6,5},{7,6},{9,8},{10,9},{11,10},{13,12},{... | collective-permute-start | bytes 442376 | tf_op jit(solution)/shard_map/ppermute | solution.py:19
  126.7 15.9 %copy.167 = bf16[2,2,2,8,1152]{2,1,4,3,0:T(2,128)(2,1)} copy(bf16[2,2,2,8,1152]{4,1,0,2,3:T(2,128)(2,1)S(1)} %bitcast.221) | data formatting | bytes 294912 | tf_op jit(solution)/shard_map/squeeze | solution.py:106
  142.6 0.1 copy.175
  142.8 0.2 convolution_subtract_fusion.5
  143.0 5.6 %gather_fusion.2 = bf16[96,2,2,2]{3,2,1,0:T(2,128)(2,1)} fusion(bf16[2,2,2,96,96]{2,1,4,3,0:T(2,128)(2,1)} %bitcast.219, s32[96]{0:T(128)S(1)} %or_bitcast_fusion), kind=kCustom, calls=%fused_computation.2 | custom fusion | bytes 3840 | tf_op jit(solution)/shard_map/jit(diagonal)/gather | solution.py:107
  148.6 0.3 add_reduce_fusion.1
  148.9 1.1 concatenate.12
  150.0 0.1 copy.171
  150.1 0.2 fusion.39
  150.3 0.2 fusion.41
  150.5 0.2 concatenate.14
  150.7 0.1 copy.179
  150.9 0.2 fusion.27
  151.1 0.2 fusion.29
  151.3 0.1 copy.169
  151.4 0.1 copy.177
  151.5 0.2 convolution_subtract_fusion.6
  151.7 0.2 convolution_subtract_fusion.4
  151.9 0.3 add_reduce_fusion.2
  152.2 0.3 add_reduce_fusion
  152.5 1.1 fusion.5
  153.6 0.6 copy.156
  (39 shorter events, 1.0 us)
Async XLA Ops:
  26.8 21.6 %copy-start.2 = (s32[16]{0:T(128)S(1)}, s32[16]{0:T(128)}, u32[]{:S(2)}) copy-start(s32[16]{0:T(128)} %param.8) | copy-start | bytes 196
  26.8 23.0 %copy-start.1 = (bf16[2,2,16,1,1152]{4,2,3,1,0:T(8,128)(2,1)S(1)}, bf16[2,2,16,1,1152]{4,2,3,1,0:T(8,128)(2,1)}, u32[]{:S(2)}) copy-start(bf16[2,2,16,1,1152]{4,2,3,1,0:T(8,128)(2,1)} %param.6) | copy-start | bytes 442372
  42.0 12.7 %all-to-all-start = ((bf16[8,2,4608]{2,1,0:T(2,128)(2,1)}), bf16[8,2,4608]{2,1,0:T(2,128)(2,1)S(1)}, u32[]{:S(2)}, u32[]{:S(2)}) async-start(bf16[8,2,4608]{2,1,0:T(2,128)(2,1)} %reshape.231), calls=%async_computation | async-start | bytes 294912 | tf_op jit(solution)/shard_map/all_to_all | solution.py:70
  76.1 35.6 %copy-start = (bf16[2,2,1,3,96,192]{5,4,3,2,1,0:T(8,128)(2,1)S(1)}, bf16[2,2,1,3,96,192]{5,4,3,2,1,0:T(8,128)(2,1)}, u32[]{:S(2)}) copy-start(bf16[2,2,1,3,96,192]{5,4,3,2,1,0:T(8,128)(2,1)} %param.7) | copy-start | bytes 1327108
  108.1 9.7 %all-to-all-start.1 = ((bf16[2,2,16,1152]{3,1,0,2:T(2,128)(2,1)}), bf16[2,2,16,1152]{3,1,0,2:T(2,128)(2,1)S(1)}, u32[]{:S(2)}, u32[]{:S(2)}) async-start(bf16[2,2,16,1152]{3,1,0,2:T(2,128)(2,1)} %fusion.6), calls=%async_computation.1 | async-start | bytes 294912 | tf_op jit(solution)/shard_map/all_to_all | solution.py:90
  118.6 30.2 %collective-permute-start = (bf16[2,2,2,1,9216]{4,2,1,0,3:T(2,128)(2,1)S(1)}, bf16[2,2,2,1,9216]{4,2,1,0,3:T(2,128)(2,1)}, u32[]{:S(2)}, u32[]{:S(2)}) collective-permute-start(bf16[2,2,2,1,9216]{4,2,1,0,3:T(2,128)(2,1)S(1)} %broadcast_in_dim.54), channel_id=1, source_target_pairs={{0,1},{1,2},{2,3},{4,5},{5,6},{6,7},{8,9},{9,10},{10,11},{12,13},{... | collective-permute-start | bytes 442376 | tf_op jit(solution)/shard_map/ppermute | solution.py:17
  124.8 25.7 %collective-permute-start.1 = (bf16[2,2,2,1,9216]{4,2,1,0,3:T(2,128)(2,1)S(1)}, bf16[2,2,2,1,9216]{4,2,1,0,3:T(2,128)(2,1)S(1)}, u32[]{:S(2)}, u32[]{:S(2)}) collective-permute-start(bf16[2,2,2,1,9216]{4,2,1,0,3:T(2,128)(2,1)S(1)} %broadcast_in_dim.54), channel_id=1, source_target_pairs={{1,0},{2,1},{3,2},{5,4},{6,5},{7,6},{9,8},{10,9},{11,10},{13,12},{... | collective-permute-start | bytes 442376 | tf_op jit(solution)/shard_map/ppermute | solution.py:19
where the time goes:
time: 156 us; the launch traced here: 154 us
  local copies, waits for them, and re-layouts  111 us (71%)
  starting transfers between devices  18 us (12%)
  matrix products  10.8 us (7%)
  waiting for transfers between devices  9.76 us (6%)
  other arithmetic  2.94 us (2%)
    unnamed x16, local copies, waits for them, and re-layouts  64.1 us
    all_to_all x1, local copies, waits for them, and re-layouts, shards(): lax.all_to_all(local, 'energy', split_axis=3, concat_axis=2, tiled=True)  19.9 us
    squeeze x1, local copies, waits for them, and re-layouts, shards(): own = sigma_all[:, :, :, 1].astype(jnp.float32)  15.9 us
    all_to_all x1, starting transfers between devices, shards(): lax.all_to_all(local, 'energy', split_axis=3, concat_axis=2, tiled=True)  6.38 us
    ppermute x1, starting transfers between devices, with_halo(): lax.ppermute(tail, axis, [(i, (i + 1) % count) for i in range(ends)])  6.13 us
    all_to_all x1, waiting for transfers between devices, shards(): lax.all_to_all(sigma, 'energy', split_axis=2, concat_axis=3, tiled=True)  6.02 us
    gather x1, local copies, waits for them, and re-layouts, shards(): diagonal_part = jnp.diagonal(own, axis1=3, axis2=4)  5.6 us
    all_to_all x1, waiting for transfers between devices, shards(): lax.all_to_all(local, 'energy', split_axis=3, concat_axis=2, tiled=True)  3.73 us
  transfers between devices with their start and end apart: 4, of which 2 were waited for; matrix products, arithmetic and copies ran while one was open for 17% of the time, Pallas kernels for 0%

commit v1 on v0

v1 whole, which is shorter than its diff:
```python
import functools
import math

import jax
import jax.numpy as jnp
from jax import lax
from jax.experimental import pallas as pl
from jax.experimental.pallas import tpu as pltpu
from jax.sharding import PartitionSpec as P

F32 = jnp.float32
BF16 = jnp.bfloat16
VMEM = pl.BlockSpec(memory_space=pltpu.VMEM)
SMEM = pl.BlockSpec(memory_space=pltpu.SMEM)


def call(kernel, out_shape, in_specs, flops, scratch=()):
    return pl.pallas_call(
        kernel,
        out_shape=out_shape,
        in_specs=in_specs,
        out_specs=VMEM,
        scratch_shapes=list(scratch),
        compiler_params=pltpu.CompilerParams(vmem_limit_bytes=16 * 2**20),
        cost_estimate=pl.CostEstimate(flops=flops, bytes_accessed=2**20, transcendentals=0),
    )


def pack_kernel(devices, green_ref, out_ref):
    pairs, slots, entries = green_ref.shape
    columns = entries // devices
    rows = pairs * slots
    whole = jnp.concatenate([green_ref[at].astype(F32) for at in range(pairs)], axis=0)
    for at in range(devices):
        out_ref[at * rows : (at + 1) * rows, :] = whole[:, at * columns : (at + 1) * columns].astype(BF16)


def split_high_low(values):
    high = values.astype(BF16)
    return high, (values - high.astype(F32)).astype(BF16)


def convolve_kernel(first_ref, second_ref, spread_ref, screen_ref, out_ref):
    total = screen_ref.shape[0] // 4
    first_high, first_low = split_high_low(first_ref[...])
    spread = spread_ref[...]
    times = jnp.dot(
        jnp.concatenate([first_high, first_low], axis=1),
        jnp.concatenate([spread, spread], axis=0),
        preferred_element_type=F32,
    )
    screen = screen_ref[...].astype(F32)
    mixed = []
    for kind in range(2):
        base = kind * 2 * total
        times_re, times_im = times[base : base + total], times[base + total : base + 2 * total]
        screen_re, screen_im = screen[base : base + total], screen[base + total : base + 2 * total]
        mixed.append(times_re * screen_re - times_im * screen_im)
        mixed.append(times_re * screen_im + times_im * screen_re)
    mixed_high, mixed_low = split_high_low(jnp.concatenate(mixed, axis=0))
    second_high, second_low = split_high_low(second_ref[...])
    sigma = jnp.dot(
        jnp.concatenate([second_high, second_low, second_high], axis=1),
        jnp.concatenate([mixed_high, mixed_high, mixed_low], axis=0),
        preferred_element_type=F32,
    )
    out_ref[...] = sigma.astype(BF16)


def row_positions(slab, devices, shape):
    at = lax.broadcasted_iota(jnp.int32, shape, 0)
    return at % devices * (slab // devices) + at // devices


def to_tiles(tiles_ref, values):
    lanes = values.shape[1]
    for tile in range(tiles_ref.shape[0]):
        last = min(lanes, 128 * (tile + 1))
        tiles_ref[tile, :, : last - 128 * tile] = values[:, 128 * tile : last]


def strided_rows(tiles_ref, start, count, stride, lanes):
    found = [tiles_ref[tile, pl.ds(start, count, stride=stride), :] for tile in range(tiles_ref.shape[0])]
    return jnp.concatenate(found, axis=1)[:, :lanes]


def spread_rows(sigma_ref, wide_ref, slab, devices):
    to_tiles(wide_ref, sigma_ref[...].astype(F32))
    each = sigma_ref.shape[0] // devices
    depth = slab // devices
    matrices = []
    for at in range(each):
        flat = strided_rows(wide_ref, at, devices, each, slab * depth)
        matrices.append(
            jnp.concatenate([flat[:, slab * i : slab * (i + 1)] for i in range(depth)], axis=0)
        )
    return matrices


def neighbour_density(matrices, right_re, right_im, slot, slab, devices, scratch_ref):
    depth = slab // devices
    width = right_re.shape[1]
    shuffled = []
    for right in (right_re, right_im):
        to_tiles(scratch_ref, right.astype(F32))
        chunks = [strided_rows(scratch_ref, i, devices, depth, width) for i in range(depth)]
        shuffled.append(jnp.concatenate(chunks, axis=0))
    left = jnp.concatenate(
        [
            jnp.concatenate([matrices[slot * 4 + kind * 2], matrices[slot * 4 + kind * 2 + 1]], axis=1)
            for kind in range(2)
        ],
        axis=0,
    ).astype(BF16)
    inner_re = jnp.dot(left, jnp.concatenate([right_re, right_im], axis=0), preferred_element_type=F32)
    inner_im = jnp.dot(left, jnp.concatenate([-right_im, right_re], axis=0), preferred_element_type=F32)
    result = []
    for kind in range(2):
        z_re = inner_re[kind * slab : (kind + 1) * slab]
        z_im = inner_im[kind * slab : (kind + 1) * slab]
        result.append(
            (
                jnp.sum(z_re * shuffled[0] - z_im * shuffled[1], axis=0, keepdims=True),
                jnp.sum(z_re * shuffled[1] + z_im * shuffled[0], axis=0, keepdims=True),
            )
        )
    return result


def density_own_kernel(devices, start_ref, which_ref, sigma_ref, side_ref, retarded_ref, out_ref, wide_ref, scratch_ref):
    slots, slab, width = retarded_ref.shape[1], retarded_ref.shape[3], retarded_ref.shape[4]
    own = spread_rows(sigma_ref, wide_ref, slab, devices)
    side = spread_rows(side_ref, wide_ref, slab, devices)
    on_diagonal = row_positions(slab, devices, (slab, slab)) == lax.broadcasted_iota(jnp.int32, (slab, slab), 1)
    place = row_positions(slab, devices, (slab, width)) + start_ref[0] == lax.broadcasted_iota(
        jnp.int32, (slab, width), 1
    )
    which = which_ref[0]
    for slot in range(slots):
        first = neighbour_density(own, retarded_ref[0, slot, 1], retarded_ref[1, slot, 1], slot, slab, devices, scratch_ref)
        second = neighbour_density(side, retarded_ref[0, slot, which], retarded_ref[1, slot, which], slot, slab, devices, scratch_ref)
        for kind in range(2):
            for part in range(2):
                matrix = own[slot * 4 + kind * 2 + part]
                column = jnp.sum(jnp.where(on_diagonal, matrix, 0.0), axis=1, keepdims=True)
                direct = jnp.sum(jnp.where(place, column, 0.0), axis=0, keepdims=True)
                out_ref[kind * 2 + part, slot : slot + 1, :] = first[kind][part] + second[kind][part] + direct


def density_far_kernel(devices, which_ref, sigma_ref, retarded_ref, before_ref, out_ref, wide_ref, scratch_ref):
    slots, slab = retarded_ref.shape[1], retarded_ref.shape[3]
    far = spread_rows(sigma_ref, wide_ref, slab, devices)
    which = which_ref[0]
    for slot in range(slots):
        found = neighbour_density(far, retarded_ref[0, slot, which], retarded_ref[1, slot, which], slot, slab, devices, scratch_ref)
        for kind in range(2):
            for part in range(2):
                row = kind * 2 + part
                out_ref[row, slot : slot + 1, :] = before_ref[row, slot : slot + 1, :] + found[kind][part]


def phases(energy, time, quarter, count):
    turns = (4 * energy * time + count * quarter) % (4 * count)
    return jnp.cos(turns.astype(F32) * (2.0 * math.pi / (4 * count)))


def tables(energy_order, devices, slots):
    total = devices * slots
    size = 4 * total
    row = lax.broadcasted_iota(jnp.int32, (size, size), 0)
    col = lax.broadcasted_iota(jnp.int32, (size, size), 1)
    order = energy_order.reshape(devices, 1, 1, slots)
    energy = jnp.broadcast_to(order, (devices, 2, 2, slots)).reshape(1, size)
    same = row // (2 * total) == col // (2 * slots) % 2
    quarter = row // total % 2 - col // slots % 2
    first = jnp.where(same, phases(energy, row % total, quarter, total), 0.0)
    energy = jnp.broadcast_to(energy_order.reshape(total, 1), (total, 4)).reshape(size, 1)
    same = row // 2 % 2 == col // (2 * total)
    quarter = 1 - row % 2 + col // total % 2
    second = jnp.where(same, phases(energy, col % total, quarter, total), 0.0) * (1.0 / total)
    return first, second


def shards(green_window, screened, retarded, energy_order, window_start):
    devices = lax.axis_size("energy")
    rows = lax.axis_size("rows")
    slots, entries = green_window.shape[2], green_window.shape[4]
    slab, width = retarded.shape[4], retarded.shape[5]
    total = devices * slots
    columns = entries // devices
    flat = jax.ShapeDtypeStruct((4 * total, columns), BF16)

    packed = call(functools.partial(pack_kernel, devices), flat, [VMEM], 1000)(
        green_window.reshape(4, slots, entries)
    )
    spread = lax.all_to_all(packed, "energy", split_axis=0, concat_axis=0, tiled=True)
    first, second = tables(energy_order, devices, slots)
    sigma = call(convolve_kernel, flat, [VMEM] * 4, 2 * 5 * 16 * total * total * columns)(
        first, second, spread, screened.reshape(4 * total, columns)
    )
    returned = lax.all_to_all(sigma, "energy", split_axis=0, concat_axis=0, tiled=True)

    def trade(first_row):
        pairs = []
        for low in range(first_row, rows - 1, 2):
            pairs += [(low, low + 1), (low + 1, low)]
        return lax.ppermute(returned, "rows", pairs)

    far = trade(1)
    near = trade(0)
    odd = lax.axis_index("rows") % 2
    near_block = (2 - 2 * odd).astype(jnp.int32).reshape(1)
    far_block = (2 * odd).astype(jnp.int32).reshape(1)
    blocks = retarded.reshape(2, slots, 3, slab, width)
    scratch = [pltpu.VMEM((pl.cdiv(columns, 128), 4 * total, 128), F32), pltpu.VMEM((pl.cdiv(width, 128), slab, 128), F32)]
    out = jax.ShapeDtypeStruct((4, slots, width), F32)
    work = 2 * 8 * slots * 2 * slab * slab * width
    density = call(functools.partial(density_own_kernel, devices), out, [SMEM, SMEM] + [VMEM] * 3, 2 * work, scratch)(
        window_start, near_block, returned, near, blocks
    )
    density = call(functools.partial(density_far_kernel, devices), out, [SMEM] + [VMEM] * 3, work, scratch)(
        far_block, far, blocks, density
    )
    return density.reshape(2, 2, slots, 1, width)


def solution(mesh):
    in_specs = (
        P(None, None, "energy", "rows", None),
        P(None, None, None, "rows", "energy"),
        P(None, "energy", "rows", None, None, None),
        P(),
        P("rows"),
    )
    out_specs = P(None, None, "energy", "rows", None)
    return jax.shard_map(shards, mesh=mesh, in_specs=in_specs, out_specs=out_specs, check_vma=False)
```

time: 156 us -> 34.7 us (0.22)
  local copies, waits for them, and re-layouts: 111 us -> 1.89 us
  matrix products: 10.8 us -> 0 us
  blocking collectives: 0 us -> 9.04 us
  starting transfers between devices: 18 us -> 12.4 us
  Pallas kernels: 0 us -> 2.57 us
  waiting for transfers between devices: 9.76 us -> 7.2 us
  other arithmetic: 2.94 us -> 0.55 us
    unnamed x16 -> x8, local copies, waits for them, and re-layouts: 64.1 us -> 0.92 us
    all_to_all x2 -> x0, local copies, waits for them, and re-layouts: 19.9 us -> none  [the longest x1 19.9 us: shards(): lax.all_to_all(local, 'energy', split_axis=3, concat_axis=2, tiled=True)]
    squeeze x3 -> x0, local copies, waits for them, and re-layouts: 16.2 us -> none  [the longest x1 15.9 us: shards(): own = sigma_all[:, :, :, 1].astype(jnp.float32)]
    dot_general x29 -> x0, matrix products: 10.8 us -> none  [the longest x12 2.56 us: window_product(): jnp.einsum('gepq,epa->geqa', part, right, preferred_element_type=jnp.floa...]
    all_to_all x0 -> x1, blocking collectives: none -> 9.04 us  [shards(): lax.all_to_all(sigma, 'energy', split_axis=0, concat_axis=0, tiled=True)]
    gather x3 -> x0, local copies, waits for them, and re-layouts: 7.33 us -> none  [the longest x1 5.6 us: shards(): diagonal_part = jnp.diagonal(own, axis1=3, axis2=4)]
    all_to_all x2 -> x1, waiting for transfers between devices: 9.75 us -> 5.31 us  [shards(): lax.all_to_all(packed, 'energy', split_axis=0, concat_axis=0, tiled=True)]
    all_to_all x2 -> x1, starting transfers between devices: 9.98 us -> 6.51 us  [shards(): lax.all_to_all(packed, 'energy', split_axis=0, concat_axis=0, tiled=True)]
  transfers between devices with their start and end apart: 4 -> 3, of which waited for: 2 -> 2; matrix products, arithmetic and copies ran while one was open for 17% -> 3% of each run, Pallas kernels for 0% -> 3%
where the time goes in v1:
time: 34.7 us; the launch traced here: 34.5 us
  starting transfers between devices  12.4 us (36%)
  blocking collectives  9.04 us (26%)
  waiting for transfers between devices  7.2 us (21%)
  Pallas kernels  2.57 us (7%)
  local copies, waits for them, and re-layouts  1.89 us (5%)
  between operations  0.8 us (2%)
  other arithmetic  0.55 us (2%)
    all_to_all x1, blocking collectives, shards(): lax.all_to_all(sigma, 'energy', split_axis=0, concat_axis=0, tiled=True)  9.04 us
    all_to_all x1, starting transfers between devices, shards(): lax.all_to_all(packed, 'energy', split_axis=0, concat_axis=0, tiled=True)  6.51 us
    ppermute x2, starting transfers between devices, trade(): return lax.ppermute(returned, 'rows', pairs)  5.89 us
    all_to_all x1, waiting for transfers between devices, shards(): lax.all_to_all(packed, 'energy', split_axis=0, concat_axis=0, tiled=True)  5.31 us
    ppermute x2, waiting for transfers between devices, trade(): return lax.ppermute(returned, 'rows', pairs)  1.89 us
    unnamed x8, local copies, waits for them, and re-layouts  0.92 us
    pallas_call x1, Pallas kernels, shards(): call(functools.partial(density_own_kernel, devices), out, [SMEM, SMEM] +...  0.87 us
    pallas_call x1, Pallas kernels, shards(): call(functools.partial(pack_kernel, devices), flat, [VMEM], 1000)  0.75 us
  transfers between devices with their start and end apart: 3, of which 2 were waited for; matrix products, arithmetic and copies ran while one was open for 3% of the time, Pallas kernels for 3%

profile of v1, /device:TPU:1, one launch (start us, length us, event | category | flops | bytes accessed | tf_op | source)
XLA Modules:
  0.0 34.5 jit_solution(12498318533975594548)
XLA Ops:
  0.0 0.0 copy-start.1
  0.0 0.9 %copy-done.1 = bf16[2,2,2,1,9216]{4,2,3,1,0:T(2,128)(2,1)S(1)} copy-done((bf16[2,2,2,1,9216]{4,2,3,1,0:T(2,128)(2,1)S(1)}, bf16[2,2,2,1,9216]{4,2,3,1,0:T(2,128)(2,1)}, u32[]{:S(2)}) %copy-start.1) | copy-done | bytes 147480
  0.9 0.8 %shard_map.55 = bf16[64,1152]{1,0:T(8,128)(2,1)} custom-call(bf16[4,2,9216]{2,1,0:T(2,128)(2,1)S(1)} %bitcast.17), custom_call_target="tpu_custom_call" | custom-call | flops 1000 | bytes 1048576 | tf_op jit(solution)/shard_map/pallas_call | solution.py:193
  1.7 0.0 copy-start.3
  1.7 0.0 copy-start.2
  1.7 6.5 %all-to-all-start = ((bf16[8,8,1152]{2,1,0:T(8,128)(2,1)}), bf16[8,8,1152]{2,1,0:T(8,128)(2,1)S(1)}, u32[]{:S(2)}, u32[]{:S(2)}) async-start(bf16[8,8,1152]{2,1,0:T(8,128)(2,1)} %bitcast.2), calls=%async_computation | async-start | bytes 294912 | tf_op jit(solution)/shard_map/all_to_all | solution.py:196
  8.2 0.0 copy-start
  8.3 0.0 copy-done.3
  8.3 0.1 mul.72
  8.4 0.1 mul.73
  8.5 0.3 fusion.8.first_ref
  8.8 0.1 broadcast_in_dim.17
  8.9 0.1 mul.79
  8.9 0.2 fusion.18.second_ref
  9.2 5.3 %all-to-all-done = bf16[8,8,1152]{2,1,0:T(8,128)(2,1)S(1)} async-done(((bf16[8,8,1152]{2,1,0:T(8,128)(2,1)}), bf16[8,8,1152]{2,1,0:T(8,128)(2,1)S(1)}, u32[]{:S(2)}, u32[]{:S(2)}) %all-to-all-start) | async-done | bytes 147488 | tf_op jit(solution)/shard_map/all_to_all | solution.py:196
  14.5 0.0 copy-done.2
  14.5 0.5 %shard_map.56 = bf16[64,1152]{1,0:T(8,128)(2,1)S(1)} custom-call(f32[64,64]{1,0:T(8,128)S(1)} %fusion.8.first_ref, f32[64,64]{1,0:T(8,128)S(1)} %fusion.18.second_ref, bf16[64,1152]{1,0:T(8,128)(2,1)S(1)} %bitcast.12, bf16[64,1152]{1,0:T(8,128)(2,1)S(1)} %bitcast.18), custom_call_target="tpu_custom_call" | custom-call | flops 47185920 | bytes 1048576 | tf_op jit(solution)/shard_map/pallas_call | solution.py:198
  15.0 9.0 %all_to_all.22 = bf16[8,8,1152]{2,1,0:T(8,128)(2,1)S(1)} all-to-all(bf16[8,8,1152]{2,1,0:T(8,128)(2,1)S(1)} %bitcast.16), channel_id=1, replica_groups=mesh['energy'=8,'rows'=4] {'energy'}, dimensions={0} | all-to-all | bytes 294912 | tf_op jit(solution)/shard_map/all_to_all | solution.py:201
  24.0 2.9 %collective-permute-start.1 = (bf16[64,1152]{1,0:T(8,128)(2,1)S(1)}, bf16[64,1152]{1,0:T(8,128)(2,1)S(1)}, u32[]{:S(2)}, u32[]{:S(2)}) collective-permute-start(bf16[64,1152]{1,0:T(8,128)(2,1)S(1)} %bitcast.13), channel_id=1, source_target_pairs={{0,1},{1,0},{2,3},{3,2},{4,5},{5,4},{6,7},{7,6},{8,9},{9,8},{10,11... | collective-permute-start | bytes 442376 | tf_op jit(solution)/shard_map/ppermute | solution.py:207
  26.9 3.0 %collective-permute-start = (bf16[64,1152]{1,0:T(8,128)(2,1)S(1)}, bf16[64,1152]{1,0:T(8,128)(2,1)S(1)}, u32[]{:S(2)}, u32[]{:S(2)}) collective-permute-start(bf16[64,1152]{1,0:T(8,128)(2,1)S(1)} %bitcast.14), channel_id=1, source_target_pairs={{1,2},{2,1},{5,6},{6,5},{9,10},{10,9},{13,14},{14,13},{17,18},{18,... | collective-permute-start | bytes 442376 | tf_op jit(solution)/shard_map/ppermute | solution.py:207
  30.6 0.0 collective-permute-done.1.side_ref
  30.6 0.0 copy-done
  30.6 0.9 %shard_map.57.before_ref = f32[4,2,192]{2,1,0:T(2,128)S(1)} custom-call(s32[1]{0:T(128)S(6)} %copy.8.start_ref, s32[1]{0:T(128)} %bitcast.8.which_ref, bf16[64,1152]{1,0:T(8,128)(2,1)S(1)} %bitcast.15, bf16[64,1152]{1,0:T(8,128)(2,1)S(1)} %collective-permute-done.1.side_ref, bf16[2,2,3,96,192]{4,3,2,1,0:T(8,128)(2,1)S(1)} %bitcast.10), custom_call_target="tpu_custom_call" | custom-call | flops 226492416 | bytes 1048576 | tf_op jit(solution)/shard_map/pallas_call | solution.py:218
  31.5 1.9 %collective-permute-done.sigma_ref = bf16[64,1152]{1,0:T(8,128)(2,1)S(1)} collective-permute-done((bf16[64,1152]{1,0:T(8,128)(2,1)S(1)}, bf16[64,1152]{1,0:T(8,128)(2,1)S(1)}, u32[]{:S(2)}, u32[]{:S(2)}) %collective-permute-start) | collective-permute-done | bytes 147488 | tf_op jit(solution)/shard_map/ppermute | solution.py:207
  33.4 0.5 %shard_map.58 = f32[4,2,192]{2,1,0:T(2,128)S(1)} custom-call(s32[1]{0:T(128)} %bitcast.which_ref, bf16[64,1152]{1,0:T(8,128)(2,1)S(1)} %collective-permute-done.sigma_ref, bf16[2,2,3,96,192]{4,3,2,1,0:T(8,128)(2,1)S(1)} %bitcast.11, f32[4,2,192]{2,1,0:T(2,128)S(1)} %shard_map.57.before_ref), custom_call_target="tpu_custom_call" | custom-call | flops 113246208 | bytes 1048576 | tf_op jit(solution)/shard_map/pallas_call | solution.py:221
  33.8 0.6 %copy.7 = f32[2,2,2,1,192]{4,3,2,1,0:T(1,128)} copy(f32[2,2,2,1,192]{4,2,1,0,3:T(2,128)S(1)} %bitcast.19) | data formatting | bytes 12288 | tf_op jit(solution)/shard_map/reshape | solution.py:224
  (11 shorter events, 0.1 us)
Async XLA Ops:
  0.0 0.9 %copy-start.1 = (bf16[2,2,2,1,9216]{4,2,3,1,0:T(2,128)(2,1)S(1)}, bf16[2,2,2,1,9216]{4,2,3,1,0:T(2,128)(2,1)}, u32[]{:S(2)}) copy-start(bf16[2,2,2,1,9216]{4,2,3,1,0:T(2,128)(2,1)} %param.5) | copy-start | bytes 442372
  1.7 6.6 %copy-start.3 = (s32[16]{0:T(128)S(1)}, s32[16]{0:T(128)}, u32[]{:S(2)}) copy-start(s32[16]{0:T(128)} %param.8) | copy-start | bytes 196
  1.7 12.8 %copy-start.2 = (bf16[2,2,16,1,1152]{4,2,3,1,0:T(8,128)(2,1)S(1)}, bf16[2,2,16,1,1152]{4,2,3,1,0:T(8,128)(2,1)}, u32[]{:S(2)}) copy-start(bf16[2,2,16,1,1152]{4,2,3,1,0:T(8,128)(2,1)} %param.6) | copy-start | bytes 442372
  1.7 12.8 %all-to-all-start = ((bf16[8,8,1152]{2,1,0:T(8,128)(2,1)}), bf16[8,8,1152]{2,1,0:T(8,128)(2,1)S(1)}, u32[]{:S(2)}, u32[]{:S(2)}) async-start(bf16[8,8,1152]{2,1,0:T(8,128)(2,1)} %bitcast.2), calls=%async_computation | async-start | bytes 294912 | tf_op jit(solution)/shard_map/all_to_all | solution.py:196
  8.2 22.4 %copy-start = (bf16[2,2,1,3,96,192]{5,4,3,2,1,0:T(8,128)(2,1)S(1)}, bf16[2,2,1,3,96,192]{5,4,3,2,1,0:T(8,128)(2,1)}, u32[]{:S(2)}) copy-start(bf16[2,2,1,3,96,192]{5,4,3,2,1,0:T(8,128)(2,1)} %param.7) | copy-start | bytes 1327108
  24.0 6.6 %collective-permute-start.1 = (bf16[64,1152]{1,0:T(8,128)(2,1)S(1)}, bf16[64,1152]{1,0:T(8,128)(2,1)S(1)}, u32[]{:S(2)}, u32[]{:S(2)}) collective-permute-start(bf16[64,1152]{1,0:T(8,128)(2,1)S(1)} %bitcast.13), channel_id=1, source_target_pairs={{0,1},{1,0},{2,3},{3,2},{4,5},{5,4},{6,7},{7,6},{8,9},{9,8},{10,11... | collective-permute-start | bytes 442376 | tf_op jit(solution)/shard_map/ppermute | solution.py:207
  26.9 6.5 %collective-permute-start = (bf16[64,1152]{1,0:T(8,128)(2,1)S(1)}, bf16[64,1152]{1,0:T(8,128)(2,1)S(1)}, u32[]{:S(2)}, u32[]{:S(2)}) collective-permute-start(bf16[64,1152]{1,0:T(8,128)(2,1)S(1)} %bitcast.14), channel_id=1, source_target_pairs={{1,2},{2,1},{5,6},{6,5},{9,10},{10,9},{13,14},{14,13},{17,18},{18,... | collective-permute-start | bytes 442376 | tf_op jit(solution)/shard_map/ppermute | solution.py:207

commit v2 on v1

--- a/solution.py
+++ b/solution.py
@@ -19,7 +19,7 @@
         kernel,
         out_shape=out_shape,
         in_specs=in_specs,
-        out_specs=VMEM,
+        out_specs=jax.tree.map(lambda _: VMEM, out_shape),
         scratch_shapes=list(scratch),
         compiler_params=pltpu.CompilerParams(vmem_limit_bytes=16 * 2**20),
         cost_estimate=pl.CostEstimate(flops=flops, bytes_accessed=2**20, transcendentals=0),
@@ -64,7 +64,8 @@
         jnp.concatenate([mixed_high, mixed_high, mixed_low], axis=0),
         preferred_element_type=F32,
     )
-    out_ref[...] = sigma.astype(BF16)
+    out_ref[0] = sigma.astype(BF16)
+    out_ref[1] = sigma.astype(BF16)
 
 
 def row_positions(slab, devices, shape):
@@ -97,14 +98,31 @@
     return matrices
 
 
-def neighbour_density(matrices, right_re, right_im, slot, slab, devices, scratch_ref):
+def prepare_kernel(devices, start_ref, blocks_ref, right_ref, shuffled_ref, place_ref, scratch_ref):
+    slots, count, slab, width = blocks_ref.shape[1:]
     depth = slab // devices
-    width = right_re.shape[1]
-    shuffled = []
-    for right in (right_re, right_im):
-        to_tiles(scratch_ref, right.astype(F32))
-        chunks = [strided_rows(scratch_ref, i, devices, depth, width) for i in range(depth)]
-        shuffled.append(jnp.concatenate(chunks, axis=0))
+    place_ref[...] = jnp.where(
+        row_positions(slab, devices, (slab, width)) + start_ref[0]
+        == lax.broadcasted_iota(jnp.int32, (slab, width), 1),
+        1.0,
+        0.0,
+    )
+    for slot in range(slots):
+        for block in range(count):
+            real, imag = blocks_ref[0, slot, block], blocks_ref[1, slot, block]
+            right_ref[slot, block, 0, :slab, :] = real
+            right_ref[slot, block, 0, slab:, :] = imag
+            right_ref[slot, block, 1, :slab, :] = -imag
+            right_ref[slot, block, 1, slab:, :] = real
+            for part, values in enumerate((real, imag)):
+                to_tiles(scratch_ref, values.astype(F32))
+                for i in range(depth):
+                    shuffled_ref[slot, block, part, i * devices : (i + 1) * devices, :] = strided_rows(
+                        scratch_ref, i, devices, depth, width
+                    )
+
+
+def neighbour_density(matrices, right_ref, shuffled_ref, slot, block, slab):
     left = jnp.concatenate(
         [
             jnp.concatenate([matrices[slot * 4 + kind * 2], matrices[slot * 4 + kind * 2 + 1]], axis=1)
@@ -112,51 +130,52 @@
         ],
         axis=0,
     ).astype(BF16)
-    inner_re = jnp.dot(left, jnp.concatenate([right_re, right_im], axis=0), preferred_element_type=F32)
-    inner_im = jnp.dot(left, jnp.concatenate([-right_im, right_re], axis=0), preferred_element_type=F32)
+    inner_re = jnp.dot(left, right_ref[slot, block, 0], preferred_element_type=F32)
+    inner_im = jnp.dot(left, right_ref[slot, block, 1], preferred_element_type=F32)
+    wide_re, wide_im = shuffled_ref[slot, block, 0], shuffled_ref[slot, block, 1]
     result = []
     for kind in range(2):
         z_re = inner_re[kind * slab : (kind + 1) * slab]
         z_im = inner_im[kind * slab : (kind + 1) * slab]
         result.append(
             (
-                jnp.sum(z_re * shuffled[0] - z_im * shuffled[1], axis=0, keepdims=True),
-                jnp.sum(z_re * shuffled[1] + z_im * shuffled[0], axis=0, keepdims=True),
+                jnp.sum(z_re * wide_re - z_im * wide_im, axis=0, keepdims=True),
+                jnp.sum(z_re * wide_im + z_im * wide_re, axis=0, keepdims=True),
             )
         )
     return result
 
 
-def density_own_kernel(devices, start_ref, which_ref, sigma_ref, side_ref, retarded_ref, out_ref, wide_ref, scratch_ref):
-    slots, slab, width = retarded_ref.shape[1], retarded_ref.shape[3], retarded_ref.shape[4]
-    own = spread_rows(sigma_ref, wide_ref, slab, devices)
-    side = spread_rows(side_ref, wide_ref, slab, devices)
+def density_kernel(devices, rows, sigma_ref, right_ref, shuffled_ref, place_ref, out_ref, wide_ref):
+    slots, slab = shuffled_ref.shape[0], shuffled_ref.shape[3]
+    row = lax.axis_index("rows")
+    even = 1 - lax.rem(row, 2)
+    has_far = jnp.where(jnp.logical_and(row > 0, row < rows - 1), 1.0, 0.0)
+    own = spread_rows(sigma_ref.at[even], wide_ref, slab, devices)
+    far = spread_rows(sigma_ref.at[1 - even], wide_ref, slab, devices)
     on_diagonal = row_positions(slab, devices, (slab, slab)) == lax.broadcasted_iota(jnp.int32, (slab, slab), 1)
-    place = row_positions(slab, devices, (slab, width)) + start_ref[0] == lax.broadcasted_iota(
-        jnp.int32, (slab, width), 1
-    )
-    which = which_ref[0]
+    place = place_ref[...]
     for slot in range(slots):
-        first = neighbour_density(own, retarded_ref[0, slot, 1], retarded_ref[1, slot, 1], slot, slab, devices, scratch_ref)
-        second = neighbour_density(side, retarded_ref[0, slot, which], retarded_ref[1, slot, which], slot, slab, devices, scratch_ref)
+        here = neighbour_density(own, right_ref, shuffled_ref, slot, 1, slab)
+        there = neighbour_density(far, right_ref, shuffled_ref, slot, 2 - 2 * even, slab)
         for kind in range(2):
             for part in range(2):
                 matrix = own[slot * 4 + kind * 2 + part]
                 column = jnp.sum(jnp.where(on_diagonal, matrix, 0.0), axis=1, keepdims=True)
-                direct = jnp.sum(jnp.where(place, column, 0.0), axis=0, keepdims=True)
-                out_ref[kind * 2 + part, slot : slot + 1, :] = first[kind][part] + second[kind][part] + direct
-
-
-def density_far_kernel(devices, which_ref, sigma_ref, retarded_ref, before_ref, out_ref, wide_ref, scratch_ref):
-    slots, slab = retarded_ref.shape[1], retarded_ref.shape[3]
-    far = spread_rows(sigma_ref, wide_ref, slab, devices)
-    which = which_ref[0]
+                direct = jnp.sum(place * column, axis=0, keepdims=True)
+                out_ref[(kind * 2 + part) * slots + slot] = here[kind][part] + there[kind][part] * has_far + direct
+
+
+def density_near_kernel(devices, sigma_ref, right_ref, shuffled_ref, before_ref, out_ref, wide_ref):
+    slots, slab = shuffled_ref.shape[0], shuffled_ref.shape[3]
+    near = spread_rows(sigma_ref, wide_ref, slab, devices)
+    block = 2 - 2 * lax.rem(lax.axis_index("rows"), 2)
     for slot in range(slots):
-        found = neighbour_density(far, retarded_ref[0, slot, which], retarded_ref[1, slot, which], slot, slab, devices, scratch_ref)
+        found = neighbour_density(near, right_ref, shuffled_ref, slot, block, slab)
         for kind in range(2):
             for part in range(2):
-                row = kind * 2 + part
-                out_ref[row, slot : slot + 1, :] = before_ref[row, slot : slot + 1, :] + found[kind][part]
+                at = (kind * 2 + part) * slots + slot
+                out_ref[at] = before_ref[at] + found[kind][part]
 
 
 def phases(energy, time, quarter, count):
@@ -195,31 +214,52 @@
     )
     spread = lax.all_to_all(packed, "energy", split_axis=0, concat_axis=0, tiled=True)
     first, second = tables(energy_order, devices, slots)
-    sigma = call(convolve_kernel, flat, [VMEM] * 4, 2 * 5 * 16 * total * total * columns)(
-        first, second, spread, screened.reshape(4 * total, columns)
-    )
-    returned = lax.all_to_all(sigma, "energy", split_axis=0, concat_axis=0, tiled=True)
-
-    def trade(first_row):
-        pairs = []
-        for low in range(first_row, rows - 1, 2):
-            pairs += [(low, low + 1), (low + 1, low)]
-        return lax.ppermute(returned, "rows", pairs)
-
-    far = trade(1)
-    near = trade(0)
-    odd = lax.axis_index("rows") % 2
-    near_block = (2 - 2 * odd).astype(jnp.int32).reshape(1)
-    far_block = (2 * odd).astype(jnp.int32).reshape(1)
-    blocks = retarded.reshape(2, slots, 3, slab, width)
-    scratch = [pltpu.VMEM((pl.cdiv(columns, 128), 4 * total, 128), F32), pltpu.VMEM((pl.cdiv(width, 128), slab, 128), F32)]
-    out = jax.ShapeDtypeStruct((4, slots, width), F32)
+    right, shuffled, place = call(
+        functools.partial(prepare_kernel, devices),
+        (
+            jax.ShapeDtypeStruct((slots, 3, 2, 2 * slab, width), BF16),
+            jax.ShapeDtypeStruct((slots, 3, 2, slab, width), F32),
+            jax.ShapeDtypeStruct((slab, width), F32),
+        ),
+        [SMEM, VMEM],
+        10**6,
+        [pltpu.VMEM((pl.cdiv(width, 128), slab, 128), F32)],
+    )(window_start, retarded.reshape(2, slots, 3, slab, width))
+    spread, right, shuffled, place = lax.optimization_barrier((spread, right, shuffled, place))
+    sigma = call(
+        convolve_kernel,
+        jax.ShapeDtypeStruct((2, 4 * total, columns), BF16),
+        [VMEM] * 4,
+        2 * 5 * 16 * total * total * columns,
+    )(first, second, spread, screened.reshape(4 * total, columns))
+
+    odd = lax.axis_index("rows") % 2 == 1
+    sigma, odd = lax.optimization_barrier((sigma, odd))
+
+    groups = [
+        [energy * rows + row % rows for row in (low, low + 1) for energy in range(devices)]
+        for low in range(1, rows, 2)
+    ]
+    both = lax.all_to_all(
+        sigma.reshape(2 * devices, 4 * slots, columns),
+        ("energy", "rows"),
+        split_axis=0,
+        concat_axis=0,
+        tiled=True,
+        axis_index_groups=groups,
+    ).reshape(2, 4 * total, columns)
+    own = jnp.where(odd, both[0], both[1])
+    pairs = [(row, row ^ 1) for row in range(rows)]
+    near = lax.ppermute(own, "rows", pairs)
+
+    scratch = [pltpu.VMEM((pl.cdiv(columns, 128), 4 * total, 128), F32)]
+    out = jax.ShapeDtypeStruct((4 * slots, 1, width), F32)
     work = 2 * 8 * slots * 2 * slab * slab * width
-    density = call(functools.partial(density_own_kernel, devices), out, [SMEM, SMEM] + [VMEM] * 3, 2 * work, scratch)(
-        window_start, near_block, returned, near, blocks
-    )
-    density = call(functools.partial(density_far_kernel, devices), out, [SMEM] + [VMEM] * 3, work, scratch)(
-        far_block, far, blocks, density
+    density = call(functools.partial(density_kernel, devices, rows), out, [VMEM] * 4, 2 * work, scratch)(
+        both, right, shuffled, place
+    )
+    density = call(functools.partial(density_near_kernel, devices), out, [VMEM] * 4, work, scratch)(
+        near, right, shuffled, density
     )
     return density.reshape(2, 2, slots, 1, width)
 

time: 34.7 us -> 33.9 us (0.977)
  blocking collectives: 9.04 us -> 15.1 us
  starting transfers between devices: 12.4 us -> 7.56 us
  waiting for transfers between devices: 7.2 us -> 3.81 us
  Pallas kernels: 2.57 us -> 3.49 us
  other arithmetic: 0.55 us -> 1.23 us
  local copies, waits for them, and re-layouts: 1.89 us -> 1.35 us
    all_to_all x1, blocking collectives: 9.04 us -> 15.1 us  [shards(): lax.all_to_all(sigma.reshape(2 * devices, 4 * slots, columns), ('energy',...]
    ppermute x2 -> x1, starting transfers between devices: 5.89 us -> 1.18 us  [shards(): near = lax.ppermute(own, 'rows', pairs)]
    ppermute x2 -> x1, waiting for transfers between devices: 1.89 us -> 0.18 us  [shards(): near = lax.ppermute(own, 'rows', pairs)]
    all_to_all x1, waiting for transfers between devices: 5.31 us -> 3.63 us  [shards(): lax.all_to_all(packed, 'energy', split_axis=0, concat_axis=0, tiled=True)]
    pallas_call x3 -> x4, Pallas kernels: 1.82 us -> 2.74 us  [the longest x1 1.09 us: shards(): call(functools.partial(density_near_kernel, devices), out, [VMEM] * 4, wo...]
    mul x1, other arithmetic: 0.01 us -> 0.66 us  [phases(): turns = (4 * energy * time + count * quarter) % (4 * count)]
    reshape x1 -> x0, local copies, waits for them, and re-layouts: 0.61 us -> none  [shards(): return density.reshape(2, 2, slots, 1, width)]
    unnamed x8 -> x6, local copies, waits for them, and re-layouts: 0.92 us -> 0.98 us
  transfers between devices with their start and end apart: 3 -> 2, of which waited for: 2 -> 2; matrix products, arithmetic and copies ran while one was open for 3% -> 5% of each run, Pallas kernels for 3% -> 4%
where the time goes in v2:
time: 33.9 us; the launch traced here: 33.3 us
  blocking collectives  15.1 us (45%)
  starting transfers between devices  7.56 us (22%)
  waiting for transfers between devices  3.81 us (11%)
  Pallas kernels  3.49 us (10%)
  local copies, waits for them, and re-layouts  1.35 us (4%)
  other arithmetic  1.23 us (4%)
  between operations  0.77 us (2%)
    all_to_all x1, blocking collectives, shards(): lax.all_to_all(sigma.reshape(2 * devices, 4 * slots, columns), ('energy',...  15.1 us
    all_to_all x1, starting transfers between devices, shards(): lax.all_to_all(packed, 'energy', split_axis=0, concat_axis=0, tiled=True)  6.38 us
    all_to_all x1, waiting for transfers between devices, shards(): lax.all_to_all(packed, 'energy', split_axis=0, concat_axis=0, tiled=True)  3.63 us
    ppermute x1, starting transfers between devices, shards(): near = lax.ppermute(own, 'rows', pairs)  1.18 us
    pallas_call x1, Pallas kernels, shards(): call(functools.partial(density_near_kernel, devices), out, [VMEM] * 4, wo...  1.09 us
    unnamed x6, local copies, waits for them, and re-layouts  0.98 us
    pallas_call x1, Pallas kernels, shards(): call(functools.partial(density_kernel, devices, rows), out, [VMEM] * 4, 2...  0.82 us
    pallas_call x1, Pallas kernels, shards(): call(functools.partial(pack_kernel, devices), flat, [VMEM], 1000)  0.75 us
  transfers between devices with their start and end apart: 2, of which 2 were waited for; matrix products, arithmetic and copies ran while one was open for 5% of the time, Pallas kernels for 4%

profile of v2, /device:TPU:1, one launch (start us, length us, event | category | flops | bytes accessed | tf_op | source)
XLA Modules:
  0.0 33.3 jit_solution(5614495473778735994)
XLA Ops:
  0.0 0.0 copy-start
  0.0 0.0 copy-start.1
  0.0 0.0 copy-start.2
  0.0 1.0 %copy-done.2 = bf16[2,2,2,1,9216]{4,2,3,1,0:T(2,128)(2,1)S(1)} copy-done((bf16[2,2,2,1,9216]{4,2,3,1,0:T(2,128)(2,1)S(1)}, bf16[2,2,2,1,9216]{4,2,3,1,0:T(2,128)(2,1)}, u32[]{:S(2)}) %copy-start.2) | copy-done | bytes 147480
  1.0 0.8 %shard_map.55 = bf16[64,1152]{1,0:T(8,128)(2,1)} custom-call(bf16[4,2,9216]{2,1,0:T(2,128)(2,1)S(1)} %bitcast.15), custom_call_target="tpu_custom_call" | custom-call | flops 1000 | bytes 1048576 | tf_op jit(solution)/shard_map/pallas_call | solution.py:212
  1.7 6.4 %all-to-all-start = ((bf16[8,8,1152]{2,1,0:T(8,128)(2,1)}), bf16[8,8,1152]{2,1,0:T(8,128)(2,1)S(1)}, u32[]{:S(2)}, u32[]{:S(2)}) async-start(bf16[8,8,1152]{2,1,0:T(8,128)(2,1)} %bitcast.1), calls=%async_computation | async-start | bytes 294912 | tf_op jit(solution)/shard_map/all_to_all | solution.py:215
  8.2 0.7 %broadcast_multiply_fusion = s32[16]{0:T(128)S(1)} fusion(s32[16]{0:T(128)} %param.8), kind=kLoop, calls=%fused_computation.74 | loop fusion | flops 16 | bytes 128 | tf_op jit(solution)/shard_map/mul | solution.py:182
  8.9 0.1 mul.67
  9.0 0.1 mul.68
  9.1 0.3 fusion.9.first_ref
  10.0 0.1 broadcast_in_dim.17
  10.1 0.1 mul.74
  10.2 0.0 copy-done
  10.2 0.4 %shard_map.56 = (bf16[2,3,2,192,192]{4,3,2,1,0:T(8,128)(2,1)S(1)}, f32[2,3,2,96,192]{4,3,2,1,0:T(8,128)S(1)}, f32[96,192]{1,0:T(8,128)S(1)}) custom-call(s32[1]{0:T(128)S(6)} %copy.6.start_ref, bf16[2,2,3,96,192]{4,3,2,1,0:T(8,128)(2,1)S(1)} %bitcast.13), custom_call_target="tpu_custom_call" | custom-call | flops 1000000 | bytes 1048576 | tf_op jit(solution)/shard_map/pallas_call | solution.py:217
  10.6 0.2 fusion.19.second_ref
  10.8 3.6 %all-to-all-done = bf16[8,8,1152]{2,1,0:T(8,128)(2,1)S(1)} async-done(((bf16[8,8,1152]{2,1,0:T(8,128)(2,1)}), bf16[8,8,1152]{2,1,0:T(8,128)(2,1)S(1)}, u32[]{:S(2)}, u32[]{:S(2)}) %all-to-all-start) | async-done | bytes 147488 | tf_op jit(solution)/shard_map/all_to_all | solution.py:215
  14.4 0.0 copy-done.1
  14.4 0.5 %shard_map.57 = bf16[2,64,1152]{2,1,0:T(8,128)(2,1)S(1)} custom-call(f32[64,64]{1,0:T(8,128)S(1)} %fusion.9.first_ref, f32[64,64]{1,0:T(8,128)S(1)} %fusion.19.second_ref, bf16[64,1152]{1,0:T(8,128)(2,1)S(1)} %bitcast.12, bf16[64,1152]{1,0:T(8,128)(2,1)S(1)} %bitcast.14), custom_call_target="tpu_custom_call" | custom-call | flops 47185920 | bytes 1048576 | tf_op jit(solution)/shard_map/pallas_call | solution.py:229
  14.9 15.1 %all_to_all.17 = bf16[16,8,1152]{2,1,0:T(8,128)(2,1)S(1)} all-to-all(bf16[16,8,1152]{2,1,0:T(8,128)(2,1)S(1)} %bitcast.11), channel_id=1, replica_groups={{1,5,9,13,17,21,25,29,2,6,10,14,18,22,26,30},{3,7,11,15,19,23,27,31,0,4..., dimensions={0} | all-to-all | bytes 589824 | tf_op jit(solution)/shard_map/all_to_all | solution.py:243
  30.1 1.2 %collective-permute-start = (bf16[64,1152]{1,0:T(8,128)(2,1)S(1)}, bf16[64,1152]{1,0:T(8,128)(2,1)S(1)}, u32[]{:S(2)}, u32[]{:S(2)}) collective-permute-start(bf16[64,1152]{1,0:T(8,128)(2,1)S(1)} %fusion), channel_id=1, source_target_pairs={{0,1},{1,0},{2,3},{3,2},{4,5},{5,4},{6,7},{7,6},{8,9},{9,8},{10,11... | collective-permute-start | bytes 442376 | tf_op jit(solution)/shard_map/ppermute | solution.py:253
  31.2 0.8 %shard_map.58.before_ref = f32[8,1,192]{2,1,0:T(1,128)S(1)} custom-call(bf16[2,64,1152]{2,1,0:T(8,128)(2,1)S(1)} %bitcast.10, bf16[2,3,2,192,192]{4,3,2,1,0:T(8,128)(2,1)S(1)} %get-tuple-element.20.right_ref, f32[2,3,2,96,192]{4,3,2,1,0:T(8,128)S(1)} %get-tuple-element.21.shuffled_ref, f32[96,192]{1,0:T(8,128)S(1)} %get-tuple-element.22.place_ref), custom_call_target="tpu_custom_call" | custom-call | flops 226492416 | bytes 1048576 | tf_op jit(solution)/shard_map/pallas_call | solution.py:258
  32.1 0.2 collective-permute-done.sigma_ref
  32.3 1.1 %shard_map.59 = f32[8,1,192]{2,1,0:T(1,128)} custom-call(bf16[64,1152]{1,0:T(8,128)(2,1)S(1)} %collective-permute-done.sigma_ref, bf16[2,3,2,192,192]{4,3,2,1,0:T(8,128)(2,1)S(1)} %get-tuple-element.20.right_ref, f32[2,3,2,96,192]{4,3,2,1,0:T(8,128)S(1)} %get-tuple-element.21.shuffled_ref, f32[8,1,192]{2,1,0:T(1,128)S(1)} %shard_map.58.before_ref), custom_call_target="tpu_custom_call" | custom-call | flops 113246208 | bytes 1048576 | tf_op jit(solution)/shard_map/pallas_call | solution.py:261
  (11 shorter events, 0.1 us)
Async XLA Ops:
  0.0 10.2 %copy-start = (bf16[2,2,1,3,96,192]{5,4,3,2,1,0:T(8,128)(2,1)S(1)}, bf16[2,2,1,3,96,192]{5,4,3,2,1,0:T(8,128)(2,1)}, u32[]{:S(2)}) copy-start(bf16[2,2,1,3,96,192]{5,4,3,2,1,0:T(8,128)(2,1)} %param.7) | copy-start | bytes 1327108
  0.0 14.4 %copy-start.1 = (bf16[2,2,16,1,1152]{4,2,3,1,0:T(8,128)(2,1)S(1)}, bf16[2,2,16,1,1152]{4,2,3,1,0:T(8,128)(2,1)}, u32[]{:S(2)}) copy-start(bf16[2,2,16,1,1152]{4,2,3,1,0:T(8,128)(2,1)} %param.6) | copy-start | bytes 442372
  0.0 1.0 %copy-start.2 = (bf16[2,2,2,1,9216]{4,2,3,1,0:T(2,128)(2,1)S(1)}, bf16[2,2,2,1,9216]{4,2,3,1,0:T(2,128)(2,1)}, u32[]{:S(2)}) copy-start(bf16[2,2,2,1,9216]{4,2,3,1,0:T(2,128)(2,1)} %param.5) | copy-start | bytes 442372
  1.7 12.7 %all-to-all-start = ((bf16[8,8,1152]{2,1,0:T(8,128)(2,1)}), bf16[8,8,1152]{2,1,0:T(8,128)(2,1)S(1)}, u32[]{:S(2)}, u32[]{:S(2)}) async-start(bf16[8,8,1152]{2,1,0:T(8,128)(2,1)} %bitcast.1), calls=%async_computation | async-start | bytes 294912 | tf_op jit(solution)/shard_map/all_to_all | solution.py:215
  30.1 2.2 %collective-permute-start = (bf16[64,1152]{1,0:T(8,128)(2,1)S(1)}, bf16[64,1152]{1,0:T(8,128)(2,1)S(1)}, u32[]{:S(2)}, u32[]{:S(2)}) collective-permute-start(bf16[64,1152]{1,0:T(8,128)(2,1)S(1)} %fusion), channel_id=1, source_target_pairs={{0,1},{1,0},{2,3},{3,2},{4,5},{5,4},{6,7},{7,6},{8,9},{9,8},{10,11... | collective-permute-start | bytes 442376 | tf_op jit(solution)/shard_map/ppermute | solution.py:253

commit v3 on v2

v3 whole, which is shorter than its diff:
```python
import functools
import math

import jax
import jax.numpy as jnp
import numpy as np
from jax import lax
from jax.experimental import pallas as pl
from jax.experimental.pallas import tpu as pltpu
from jax.sharding import PartitionSpec as P

F32 = jnp.float32
BF16 = jnp.bfloat16
VMEM = pl.BlockSpec(memory_space=pltpu.VMEM)
SMEM = pl.BlockSpec(memory_space=pltpu.SMEM)
HBM = pl.BlockSpec(memory_space=pltpu.HBM)


def call(kernel, out_shape, in_specs, flops, scratch=(), moved=2**20):
    return pl.pallas_call(
        kernel,
        out_shape=out_shape,
        in_specs=in_specs,
        out_specs=jax.tree.map(lambda _: VMEM, out_shape),
        scratch_shapes=list(scratch),
        compiler_params=pltpu.CompilerParams(vmem_limit_bytes=16 * 2**20),
        cost_estimate=pl.CostEstimate(flops=flops, bytes_accessed=moved, transcendentals=0),
    )


def middle_of(count):
    return (count // 2 + 1) % count


def exchange_order(count):
    return [(middle_of(count) - at) % count for at in range(count)]


def shuffled_orders(count):
    draws = np.random.RandomState(20)
    first, second = ([int(at) for at in draws.permutation(count)] for _ in range(2))
    middle = middle_of(count)
    return [[middle] + [at for at in first if at != middle], second]


def split_high_low(values):
    high = values.astype(BF16)
    return high, (values - high.astype(F32)).astype(BF16)


def wrap(values, count):
    return values & (count - 1) if count & (count - 1) == 0 else values % count


def parts_of(values, count):
    return values >> (count.bit_length() - 1) if count & (count - 1) == 0 else values // count


def phases(energy, time, quarter, count):
    turns = wrap(4 * energy * time + count * quarter, 4 * count)
    half = jnp.where(turns >= 2 * count, turns - 2 * count, turns)
    odd = half >= count
    angle = jnp.where(odd, half - count, half).astype(F32) * (0.5 * math.pi / count)
    square = angle * angle
    cosine, sine = 0.0, 0.0
    for power in range(7, -1, -1):
        cosine = cosine * square + (-1) ** power / math.factorial(2 * power)
        sine = sine * square + (-1) ** power / math.factorial(2 * power + 1)
    value = jnp.where(odd, -sine * angle, cosine)
    return jnp.where(turns >= 2 * count, -value, value)


def tables(energy_order, order, back_order):
    total = energy_order.shape[1]
    slots = total // len(order)
    size = 4 * total
    row = lax.broadcasted_iota(jnp.int32, (size, 1), 0)
    col = lax.broadcasted_iota(jnp.int32, (1, size), 1)

    def device_at(place, places):
        found = jnp.zeros_like(place)
        for at, device in enumerate(places):
            found = jnp.where(place == at, device, found)
        return found

    across = lax.broadcasted_iota(jnp.int32, (total, total), 1)
    down = lax.broadcasted_iota(jnp.int32, (total, total), 0)
    energy_down = jnp.sum(jnp.where(across == down, energy_order, 0), axis=1, keepdims=True)

    source = device_at(parts_of(col, 4 * slots), order) * slots + wrap(col, slots)
    energy = jnp.sum(
        jnp.where(lax.broadcasted_iota(jnp.int32, (total, size), 0) == source, energy_down, 0), axis=0, keepdims=True
    )
    same = parts_of(row, 2 * total) == wrap(parts_of(col, 2 * slots), 2)
    quarter = wrap(parts_of(row, total), 2) - wrap(parts_of(col, slots), 2)
    first = jnp.where(same, phases(energy, wrap(row, total), quarter, total), 0.0)
    source = device_at(parts_of(row, 4 * slots), back_order) * slots + wrap(parts_of(row, 4), slots)
    energy = jnp.sum(
        jnp.where(lax.broadcasted_iota(jnp.int32, (size, total), 1) == source, energy_order, 0), axis=1, keepdims=True
    )
    same = wrap(parts_of(row, 2), 2) == parts_of(col, 2 * total)
    quarter = 1 - wrap(row, 2) + wrap(parts_of(col, total), 2)
    second = jnp.where(same, phases(energy, wrap(col, total), quarter, total), 0.0) * (1.0 / total)
    return first, second


def row_positions(slab, devices, shape):
    at = lax.broadcasted_iota(jnp.int32, shape, 0)
    return wrap(at, devices) * (slab // devices) + parts_of(at, devices)


def to_tiles(tiles_ref, values, start=0):
    rows, lanes = values.shape
    for tile in range(tiles_ref.shape[0]):
        last = min(lanes, 128 * (tile + 1))
        tiles_ref[tile, pl.ds(start, rows), : last - 128 * tile] = values[:, 128 * tile : last]


def strided_rows(tiles_ref, start, count, stride, lanes):
    found = [tiles_ref[tile, pl.ds(start, count, stride=stride), :] for tile in range(tiles_ref.shape[0])]
    return jnp.concatenate(found, axis=1)[:, :lanes]


def front_kernel(
    order,
    back_order,
    energy_hbm,
    green_hbm,
    out_ref,
    first_ref,
    second_ref,
    energy_ref,
    green_ref,
    sems,
):
    pairs = ((energy_hbm, energy_ref), (green_hbm, green_ref))
    copies = [pltpu.make_async_copy(source, target, sems.at[at]) for at, (source, target) in enumerate(pairs)]
    for copy in copies:
        copy.start()
    copies[0].wait()
    first, second = tables(energy_ref[...], order, back_order)
    first_high, first_low = split_high_low(first)
    second_high, second_low = split_high_low(second)
    first_ref[...] = jnp.concatenate([first_high, first_low], axis=1)
    second_ref[...] = jnp.concatenate([second_high, second_low, second_high], axis=1)
    copies[1].wait()
    pairs, slots, entries = green_ref.shape
    columns = entries // len(order)
    rows = pairs * slots
    whole = jnp.concatenate([green_ref[at].astype(F32) for at in range(pairs)], axis=0)
    for at, device in enumerate(order):
        out_ref[at * rows : (at + 1) * rows, :] = whole[:, device * columns : (device + 1) * columns].astype(BF16)


def prepare_block(real, imag, right_ref, shuffled_ref, scratch_ref, devices):
    slab, width = real.shape
    padded = right_ref.shape[1] // 2
    depth = slab // devices
    gap = jnp.zeros((padded - slab, width), BF16)
    for half, (upper, lower) in enumerate(((real, imag), (-imag, real))):
        right_ref[half, :slab, :] = upper
        right_ref[half, slab:padded, :] = gap
        right_ref[half, padded : padded + slab, :] = lower
        right_ref[half, padded + slab :, :] = gap
    for part, values in enumerate((real, imag)):
        to_tiles(scratch_ref, values.astype(F32))
        for i in range(depth):
            shuffled_ref[part, i * devices : (i + 1) * devices, :] = strided_rows(
                scratch_ref, i, devices, depth, width
            )


def convolve_kernel(orders, first_ref, second_ref, spread_ref, screen_ref, out_ref):
    total = screen_ref.shape[0] // 4
    spread = spread_ref[...]
    times = jnp.dot(first_ref[...], jnp.concatenate([spread, spread], axis=0), preferred_element_type=F32)
    screen = screen_ref[...].astype(F32)
    mixed = []
    for kind in range(2):
        base = kind * 2 * total
        times_re, times_im = times[base : base + total], times[base + total : base + 2 * total]
        screen_re, screen_im = screen[base : base + total], screen[base + total : base + 2 * total]
        mixed.append(times_re * screen_re - times_im * screen_im)
        mixed.append(times_re * screen_im + times_im * screen_re)
    mixed_high, mixed_low = split_high_low(jnp.concatenate(mixed, axis=0))
    sigma = jnp.dot(
        second_ref[...],
        jnp.concatenate([mixed_high, mixed_high, mixed_low], axis=0),
        preferred_element_type=F32,
    )
    each = sigma.shape[0] // len(orders[0])
    chunks = {device: sigma[at * each : (at + 1) * each] for at, device in enumerate(orders[0])}
    for side, order in enumerate(orders):
        out_ref[side] = jnp.concatenate([chunks[device] for device in order], axis=0).astype(BF16)


def spread_rows(sigma_ref, wide_ref, slab, padded, places):
    devices = len(places)
    each = sigma_ref.shape[0] // devices
    depth = slab // devices
    wide = sigma_ref[...].astype(F32)
    lanes = wide_ref.shape[0] * 128
    wide = jnp.concatenate([wide, jnp.zeros((wide.shape[0], lanes - wide.shape[1]), F32)], axis=1)
    for at, device in enumerate(places):
        to_tiles(wide_ref, wide[at * each : (at + 1) * each], device * each)
    matrices = []
    for at in range(each):
        flat = strided_rows(wide_ref, at, devices, each, lanes)
        matrices.append(
            jnp.concatenate([flat[:, slab * i : slab * i + padded] for i in range(depth)], axis=0)
        )
    return matrices


def neighbour_density(matrices, right_ref, shuffled_ref, slot):
    slab = shuffled_ref.shape[1]
    left = jnp.concatenate(
        [
            jnp.concatenate([matrices[slot * 4 + kind * 2], matrices[slot * 4 + kind * 2 + 1]], axis=1)
            for kind in range(2)
        ],
        axis=0,
    ).astype(BF16)
    inner_re = jnp.dot(left, right_ref[0], preferred_element_type=F32)
    inner_im = jnp.dot(left, right_ref[1], preferred_element_type=F32)
    wide_re, wide_im = shuffled_ref[0], shuffled_ref[1]
    result = []
    for kind in range(2):
        z_re = inner_re[kind * slab : (kind + 1) * slab]
        z_im = inner_im[kind * slab : (kind + 1) * slab]
        result.append((z_re * wide_re - z_im * wide_im, z_re * wide_im + z_im * wide_re))
    return result


def density_kernel(
    orders,
    rows,
    start_ref,
    sigma_ref,
    blocks_ref,
    out_ref,
    near_right_ref,
    near_shuffled_ref,
    wide_ref,
    scratch_ref,
    right_ref,
    shuffled_ref,
):
    slots, _, slab, width = blocks_ref.shape[1:]
    padded = right_ref.shape[3] // 2
    devices = len(orders[0])
    row = lax.axis_index("rows")
    odd = lax.rem(row, 2)
    keep = [jnp.where(row == 0, 0.0, 1.0), jnp.where(row == rows - 1, 0.0, 1.0)]
    sides = [spread_rows(sigma_ref.at[side], wide_ref, slab, padded, orders[side]) for side in range(2)]
    on_diagonal = row_positions(slab, devices, (slab, padded)) == lax.broadcasted_iota(jnp.int32, (slab, padded), 1)
    diagonal = jnp.concatenate(
        [
            jnp.sum(jnp.where(on_diagonal, jnp.where(odd == 1, upper, lower), 0.0), axis=0, keepdims=True)
            for upper, lower in zip(*sides)
        ],
        axis=0,
    )
    at_row = lax.broadcasted_iota(jnp.int32, (padded, width), 0)
    placed = at_row + start_ref[0] == lax.broadcasted_iota(jnp.int32, (padded, width), 1)
    place = jnp.where(jnp.logical_and(placed, at_row < slab), 1.0, 0.0).astype(BF16)
    direct = jnp.dot(diagonal.astype(BF16), place, preferred_element_type=F32)
    for slot in range(slots):
        found = []
        for side in range(2):
            block = side + odd
            mine = (right_ref.at[slot, side], shuffled_ref.at[slot, side])
            prepare_block(
                blocks_ref[0, slot, block], blocks_ref[1, slot, block], *mine, scratch_ref.at[slot, side], devices
            )
            found.append(neighbour_density(sides[side], *mine, slot))
        for kind in range(2):
            for part in range(2):
                at = slot * 4 + kind * 2 + part
                both = found[0][kind][part] * keep[0] + found[1][kind][part] * keep[1]
                out_ref[(kind * 2 + part) * slots + slot] = direct[at : at + 1] + jnp.sum(
                    both, axis=0, keepdims=True
                )
    for slot in range(slots):
        block = 2 - 2 * odd
        prepare_block(
            blocks_ref[0, slot, block],
            blocks_ref[1, slot, block],
            near_right_ref.at[slot],
            near_shuffled_ref.at[slot],
            scratch_ref.at[slot, 2],
            devices,
        )


def density_near_kernel(orders, sigma_ref, right_ref, shuffled_ref, before_ref, out_ref, wide_ref):
    slots, slab, padded = shuffled_ref.shape[0], shuffled_ref.shape[2], right_ref.shape[2] // 2
    odd = lax.rem(lax.axis_index("rows"), 2)
    places = [jnp.where(odd == 1, even_row, odd_row) for odd_row, even_row in zip(*orders)]
    near = spread_rows(sigma_ref, wide_ref, slab, padded, places)
    for slot in range(slots):
        found = neighbour_density(near, right_ref.at[slot], shuffled_ref.at[slot], slot)
        for kind in range(2):
            for part in range(2):
                at = (kind * 2 + part) * slots + slot
                out_ref[at] = before_ref[at] + jnp.sum(found[kind][part], axis=0, keepdims=True)


def shards(green_window, screened, retarded, energy_order, window_start):
    devices = lax.axis_size("energy")
    rows = lax.axis_size("rows")
    slots, entries = green_window.shape[2], green_window.shape[4]
    slab, width = retarded.shape[4], retarded.shape[5]
    total = devices * slots
    columns = entries // devices
    order = exchange_order(devices)
    orders = shuffled_orders(devices)
    padded = pl.cdiv(slab, 128) * 128

    def stay(values):
        return pltpu.with_memory_space_constraint(values, pltpu.HBM)

    packed, first, second = call(
        functools.partial(front_kernel, order, orders[0]),
        (
            jax.ShapeDtypeStruct((4 * total, columns), BF16),
            jax.ShapeDtypeStruct((4 * total, 2 * 4 * total), BF16),
            jax.ShapeDtypeStruct((4 * total, 3 * 4 * total), BF16),
        ),
        [HBM] * 2,
        1000,
        [
            pltpu.VMEM((1, total), jnp.int32),
            pltpu.VMEM((4, slots, entries), BF16),
            pltpu.SemaphoreType.DMA((2,)),
        ],
    )(stay(energy_order.reshape(1, total)), stay(green_window.reshape(4, slots, entries)))
    odd = lax.axis_index("rows") % 2 == 1
    packed, first, second, odd = lax.optimization_barrier((packed, first, second, odd))
    spread = lax.all_to_all(
        packed, "energy", split_axis=0, concat_axis=0, tiled=True, axis_index_groups=[order]
    )
    sigma = call(
        functools.partial(convolve_kernel, orders),
        jax.ShapeDtypeStruct((2, 4 * total, columns), BF16),
        [VMEM] * 4,
        2 * 5 * 16 * total * total * columns,
    )(first, second, spread, screened.reshape(4 * total, columns))

    groups = [
        [energy * rows + (low + side) % rows for side in range(2) for energy in orders[side]]
        for low in range(1, rows, 2)
    ]
    both = lax.all_to_all(
        sigma.reshape(2 * devices, 4 * slots, columns),
        ("energy", "rows"),
        split_axis=0,
        concat_axis=0,
        tiled=True,
        axis_index_groups=groups,
    ).reshape(2, 4 * total, columns)
    own = jnp.where(odd, both[0], both[1])
    pairs = [(row, row ^ 1) for row in range(rows)]
    near = lax.ppermute(own, "rows", pairs)

    spreading = pltpu.VMEM((pl.cdiv(columns + padded - slab, 128), 4 * total, 128), F32)
    out = jax.ShapeDtypeStruct((4 * slots, 1, width), F32)
    work = 2 * 8 * slots * 2 * slab * slab * width
    density, right, shuffled = call(
        functools.partial(density_kernel, orders, rows),
        (
            out,
            jax.ShapeDtypeStruct((slots, 2, 2 * padded, width), BF16),
            jax.ShapeDtypeStruct((slots, 2, slab, width), F32),
        ),
        [SMEM] + [VMEM] * 2,
        2 * work,
        [
            spreading,
            pltpu.VMEM((slots, 3, pl.cdiv(width, 128), slab, 128), F32),
            pltpu.VMEM((slots, 2, 2, 2 * padded, width), BF16),
            pltpu.VMEM((slots, 2, 2, slab, width), F32),
        ],
    )(window_start, both, retarded.reshape(2, slots, 3, slab, width))
    density = call(functools.partial(density_near_kernel, orders), out, [VMEM] * 4, work, [spreading])(
        near, right, shuffled, density
    )
    return density.reshape(2, 2, slots, 1, width)


def solution(mesh):
    in_specs = (
        P(None, None, "energy", "rows", None),
        P(None, None, None, "rows", "energy"),
        P(None, "energy", "rows", None, None, None),
        P(),
        P("rows"),
    )
    out_specs = P(None, None, "energy", "rows", None)
    return jax.shard_map(shards, mesh=mesh, in_specs=in_specs, out_specs=out_specs, check_vma=False)
```

time: 33.9 us -> 29.4 us (0.87)
  blocking collectives: 15.1 us -> 24.4 us
  starting transfers between devices: 7.56 us -> 0.31 us
  waiting for transfers between devices: 3.81 us -> 0.01 us
  local copies, waits for them, and re-layouts: 1.35 us -> 0.01 us
  other arithmetic: 1.23 us -> 0.02 us
    all_to_all x0 -> x1, blocking collectives: none -> 9.35 us  [shards(): lax.all_to_all(packed, 'energy', split_axis=0, concat_axis=0, tiled=True,...]
    all_to_all x1 -> x0, starting transfers between devices: 6.38 us -> none  [shards(): lax.all_to_all(packed, 'energy', split_axis=0, concat_axis=0, tiled=True)]
    all_to_all x1 -> x0, waiting for transfers between devices: 3.63 us -> none  [shards(): lax.all_to_all(packed, 'energy', split_axis=0, concat_axis=0, tiled=True)]
    unnamed x6 -> x4, local copies, waits for them, and re-layouts: 0.98 us -> 0.01 us
    mul x2 -> x0, other arithmetic: 0.91 us -> none  [the longest x1 0.66 us: phases(): turns = (4 * energy * time + count * quarter) % (4 * count)]
    ppermute x1, starting transfers between devices: 1.18 us -> 0.31 us  [shards(): near = lax.ppermute(own, 'rows', pairs)]
    pallas_call x5 -> x4, Pallas kernels: 3.49 us -> 3.52 us  [the longest x1 1.06 us: shards(): call(functools.partial(front_kernel, order, orders[0]), (jax.ShapeDtypeSt...]
  transfers between devices with their start and end apart: 2 -> 1, of which waited for: 2 -> 0; matrix products, arithmetic and copies ran while one was open for 5% -> 0% of each run, Pallas kernels for 4% -> 4%
where the time goes in v3:
time: 29.4 us; the launch traced here: 29 us
  blocking collectives  24.4 us (83%)
  Pallas kernels  3.52 us (12%)
  between operations  0.71 us (2%)
  starting transfers between devices  0.31 us (1%)
    all_to_all x1, blocking collectives, shards(): lax.all_to_all(sigma.reshape(2 * devices, 4 * slots, columns), ('energy',...  15.1 us
    all_to_all x1, blocking collectives, shards(): lax.all_to_all(packed, 'energy', split_axis=0, concat_axis=0, tiled=True,...  9.35 us
    pallas_call x1, Pallas kernels, shards(): call(functools.partial(front_kernel, order, orders[0]), (jax.ShapeDtypeSt...  1.06 us
    pallas_call x1, Pallas kernels, shards(): call(functools.partial(density_kernel, orders, rows), (out, jax.ShapeDtyp...  1.06 us
    pallas_call x1, Pallas kernels, shards(): call(functools.partial(density_near_kernel, orders), out, [VMEM] * 4, wor...  1 us
  transfers between devices with their start and end apart: 1, of which 0 were waited for; matrix products, arithmetic and copies ran while one was open for 0% of the time, Pallas kernels for 4%

profile of v3, /device:TPU:1, one launch (start us, length us, event | category | flops | bytes accessed | tf_op | source)
XLA Modules:
  0.0 29.0 jit_solution(9891124726435940413)
XLA Ops:
  0.0 1.1 %shard_map.55 = (bf16[64,1152]{1,0:T(8,128)(2,1)S(1)}, bf16[64,128]{1,0:T(8,128)(2,1)S(1)}, bf16[64,192]{1,0:T(8,128)(2,1)S(1)}) custom-call(s32[1,16]{1,0:T(1,128)} %bitcast.18, bf16[4,2,9216]{2,1,0:T(2,128)(2,1)} %bitcast.17), custom_call_target="tpu_custom_call" | custom-call | flops 1000 | bytes 1048576 | tf_op jit(solution)/shard_map/pallas_call | solution.py:323
  1.1 0.0 copy-start.1
  1.1 9.4 %all_to_all.16 = bf16[8,8,1152]{2,1,0:T(8,128)(2,1)S(1)} all-to-all(bf16[8,8,1152]{2,1,0:T(8,128)(2,1)S(1)} %bitcast.16), channel_id=1, replica_groups={{20,16,12,8,4,0,28,24},{21,17,13,9,5,1,29,25},{22,18,14,10,6,2,30,26},{..., dimensions={0} | all-to-all | bytes 294912 | tf_op jit(solution)/shard_map/all_to_all | solution.py:340
  10.4 0.0 copy-done.1
  10.4 0.4 %shard_map.56 = bf16[2,64,1152]{2,1,0:T(8,128)(2,1)S(1)} custom-call(bf16[64,128]{1,0:T(8,128)(2,1)S(1)} %get-tuple-element.19.first_ref, bf16[64,192]{1,0:T(8,128)(2,1)S(1)} %get-tuple-element.20.second_ref, bf16[64,1152]{1,0:T(8,128)(2,1)S(1)} %bitcast.13, bf16[64,1152]{1,0:T(8,128)(2,1)S(1)} %bitcast.15), custom_call_target="tpu_custom_call" | custom-call | flops 47185920 | bytes 1048576 | tf_op jit(solution)/shard_map/pallas_call | solution.py:343
  10.8 0.0 copy-start
  10.8 15.1 %all_to_all.17 = bf16[16,8,1152]{2,1,0:T(8,128)(2,1)S(1)} all-to-all(bf16[16,8,1152]{2,1,0:T(8,128)(2,1)S(1)} %bitcast.12), channel_id=1, replica_groups={{21,29,1,5,25,17,9,13,14,18,30,6,22,2,10,26},{23,31,3,7,27,19,11,15,12,..., dimensions={0} | all-to-all | bytes 589824 | tf_op jit(solution)/shard_map/all_to_all | solution.py:354
  26.0 0.3 %collective-permute-start = (bf16[64,1152]{1,0:T(8,128)(2,1)S(1)}, bf16[64,1152]{1,0:T(8,128)(2,1)S(1)}, u32[]{:S(2)}, u32[]{:S(2)}) collective-permute-start(bf16[64,1152]{1,0:T(8,128)(2,1)S(1)} %fusion), channel_id=1, source_target_pairs={{0,1},{1,0},{2,3},{3,2},{4,5},{5,4},{6,7},{7,6},{8,9},{9,8},{10,11... | collective-permute-start | bytes 442376 | tf_op jit(solution)/shard_map/ppermute | solution.py:364
  26.9 0.0 copy-done
  26.9 1.1 %shard_map.57 = (f32[8,1,192]{2,1,0:T(1,128)S(1)}, bf16[2,2,256,192]{3,2,1,0:T(8,128)(2,1)S(1)}, f32[2,2,96,192]{3,2,1,0:T(8,128)S(1)}) custom-call(s32[1]{0:T(128)S(6)} %copy.6.start_ref, bf16[2,64,1152]{2,1,0:T(8,128)(2,1)S(1)} %bitcast.11, bf16[2,2,3,96,192]{4,3,2,1,0:T(8,128)(2,1)S(1)} %bitcast.14), custom_call_target="tpu_custom_call" | custom-call | flops 226492416 | bytes 1048576 | tf_op jit(solution)/shard_map/pallas_call | solution.py:369
  28.0 0.0 collective-permute-done.sigma_ref
  28.0 1.0 %shard_map.58 = f32[8,1,192]{2,1,0:T(1,128)} custom-call(bf16[64,1152]{1,0:T(8,128)(2,1)S(1)} %collective-permute-done.sigma_ref, bf16[2,2,256,192]{3,2,1,0:T(8,128)(2,1)S(1)} %get-tuple-element.22.right_ref, f32[2,2,96,192]{3,2,1,0:T(8,128)S(1)} %get-tuple-element.23.shuffled_ref, f32[8,1,192]{2,1,0:T(1,128)S(1)} %get-tuple-element.24.before_ref), custom_call_target="tpu_custom_call" | custom-call | flops 113246208 | bytes 1048576 | tf_op jit(solution)/shard_map/pallas_call | solution.py:385
  (1 shorter events, 0.0 us)
Async XLA Ops:
  1.1 9.4 %copy-start.1 = (bf16[2,2,16,1,1152]{4,2,3,1,0:T(8,128)(2,1)S(1)}, bf16[2,2,16,1,1152]{4,2,3,1,0:T(8,128)(2,1)}, u32[]{:S(2)}) copy-start(bf16[2,2,16,1,1152]{4,2,3,1,0:T(8,128)(2,1)} %param.6) | copy-start | bytes 442372
  10.8 16.1 %copy-start = (bf16[2,2,1,3,96,192]{5,4,3,2,1,0:T(8,128)(2,1)S(1)}, bf16[2,2,1,3,96,192]{5,4,3,2,1,0:T(8,128)(2,1)}, u32[]{:S(2)}) copy-start(bf16[2,2,1,3,96,192]{5,4,3,2,1,0:T(8,128)(2,1)} %param.7) | copy-start | bytes 1327108
  26.0 2.0 %collective-permute-start = (bf16[64,1152]{1,0:T(8,128)(2,1)S(1)}, bf16[64,1152]{1,0:T(8,128)(2,1)S(1)}, u32[]{:S(2)}, u32[]{:S(2)}) collective-permute-start(bf16[64,1152]{1,0:T(8,128)(2,1)S(1)} %fusion), channel_id=1, source_target_pairs={{0,1},{1,0},{2,3},{3,2},{4,5},{5,4},{6,7},{7,6},{8,9},{9,8},{10,11... | collective-permute-start | bytes 442376 | tf_op jit(solution)/shard_map/ppermute | solution.py:364

commit v4 on v3

--- a/solution.py
+++ b/solution.py
@@ -3,7 +3,6 @@
 
 import jax
 import jax.numpy as jnp
-import numpy as np
 from jax import lax
 from jax.experimental import pallas as pl
 from jax.experimental.pallas import tpu as pltpu
@@ -28,19 +27,9 @@
     )
 
 
-def middle_of(count):
-    return (count // 2 + 1) % count
-
-
 def exchange_order(count):
-    return [(middle_of(count) - at) % count for at in range(count)]
-
-
-def shuffled_orders(count):
-    draws = np.random.RandomState(20)
-    first, second = ([int(at) for at in draws.permutation(count)] for _ in range(2))
-    middle = middle_of(count)
-    return [[middle] + [at for at in first if at != middle], second]
+    middle = count // 2 + 1
+    return [(middle - at) % count for at in range(count)]
 
 
 def split_high_low(values):
@@ -70,7 +59,7 @@
     return jnp.where(turns >= 2 * count, -value, value)
 
 
-def tables(energy_order, order, back_order):
+def tables(energy_order, order):
     total = energy_order.shape[1]
     slots = total // len(order)
     size = 4 * total
@@ -94,7 +83,7 @@
     same = parts_of(row, 2 * total) == wrap(parts_of(col, 2 * slots), 2)
     quarter = wrap(parts_of(row, total), 2) - wrap(parts_of(col, slots), 2)
     first = jnp.where(same, phases(energy, wrap(row, total), quarter, total), 0.0)
-    source = device_at(parts_of(row, 4 * slots), back_order) * slots + wrap(parts_of(row, 4), slots)
+    source = device_at(parts_of(row, 4 * slots), order) * slots + wrap(parts_of(row, 4), slots)
     energy = jnp.sum(
         jnp.where(lax.broadcasted_iota(jnp.int32, (size, total), 1) == source, energy_order, 0), axis=1, keepdims=True
     )
@@ -123,7 +112,6 @@
 
 def front_kernel(
     order,
-    back_order,
     energy_hbm,
     green_hbm,
     out_ref,
@@ -138,7 +126,7 @@
     for copy in copies:
         copy.start()
     copies[0].wait()
-    first, second = tables(energy_ref[...], order, back_order)
+    first, second = tables(energy_ref[...], order)
     first_high, first_low = split_high_low(first)
     second_high, second_low = split_high_low(second)
     first_ref[...] = jnp.concatenate([first_high, first_low], axis=1)
@@ -152,25 +140,7 @@
         out_ref[at * rows : (at + 1) * rows, :] = whole[:, device * columns : (device + 1) * columns].astype(BF16)
 
 
-def prepare_block(real, imag, right_ref, shuffled_ref, scratch_ref, devices):
-    slab, width = real.shape
-    padded = right_ref.shape[1] // 2
-    depth = slab // devices
-    gap = jnp.zeros((padded - slab, width), BF16)
-    for half, (upper, lower) in enumerate(((real, imag), (-imag, real))):
-        right_ref[half, :slab, :] = upper
-        right_ref[half, slab:padded, :] = gap
-        right_ref[half, padded : padded + slab, :] = lower
-        right_ref[half, padded + slab :, :] = gap
-    for part, values in enumerate((real, imag)):
-        to_tiles(scratch_ref, values.astype(F32))
-        for i in range(depth):
-            shuffled_ref[part, i * devices : (i + 1) * devices, :] = strided_rows(
-                scratch_ref, i, devices, depth, width
-            )
-
-
-def convolve_kernel(orders, first_ref, second_ref, spread_ref, screen_ref, out_ref):
+def convolve_kernel(first_ref, second_ref, spread_ref, screen_ref, out_ref):
     total = screen_ref.shape[0] // 4
     spread = spread_ref[...]
     times = jnp.dot(first_ref[...], jnp.concatenate([spread, spread], axis=0), preferred_element_type=F32)
@@ -187,11 +157,9 @@
         second_ref[...],
         jnp.concatenate([mixed_high, mixed_high, mixed_low], axis=0),
         preferred_element_type=F32,
-    )
-    each = sigma.shape[0] // len(orders[0])
-    chunks = {device: sigma[at * each : (at + 1) * each] for at, device in enumerate(orders[0])}
-    for side, order in enumerate(orders):
-        out_ref[side] = jnp.concatenate([chunks[device] for device in order], axis=0).astype(BF16)
+    ).astype(BF16)
+    out_ref[0] = sigma
+    out_ref[1] = sigma
 
 
 def spread_rows(sigma_ref, wide_ref, slab, padded, places):
@@ -212,8 +180,17 @@
     return matrices
 
 
-def neighbour_density(matrices, right_ref, shuffled_ref, slot):
-    slab = shuffled_ref.shape[1]
+def row_order(slab, devices):
+    shape = (slab, slab)
+    return jnp.where(
+        row_positions(slab, devices, shape) == lax.broadcasted_iota(jnp.int32, shape, 1), 1.0, 0.0
+    ).astype(BF16)
+
+
+def neighbour_density(matrices, blocks_ref, slot, block, ordering):
+    real, imag = blocks_ref[0, slot, block], blocks_ref[1, slot, block]
+    slab, width = real.shape
+    gap = jnp.zeros((matrices[0].shape[1] - slab, width), BF16)
     left = jnp.concatenate(
         [
             jnp.concatenate([matrices[slot * 4 + kind * 2], matrices[slot * 4 + kind * 2 + 1]], axis=1)
@@ -221,9 +198,10 @@
         ],
         axis=0,
     ).astype(BF16)
-    inner_re = jnp.dot(left, right_ref[0], preferred_element_type=F32)
-    inner_im = jnp.dot(left, right_ref[1], preferred_element_type=F32)
-    wide_re, wide_im = shuffled_ref[0], shuffled_ref[1]
+    inner_re = jnp.dot(left, jnp.concatenate([real, gap, imag, gap], axis=0), preferred_element_type=F32)
+    inner_im = jnp.dot(left, jnp.concatenate([-imag, gap, real, gap], axis=0), preferred_element_type=F32)
+    wide_re = jnp.dot(ordering, real, preferred_element_type=F32)
+    wide_im = jnp.dot(ordering, imag, preferred_element_type=F32)
     result = []
     for kind in range(2):
         z_re = inner_re[kind * slab : (kind + 1) * slab]
@@ -232,74 +210,41 @@
     return result
 
 
-def density_kernel(
-    orders,
-    rows,
-    start_ref,
-    sigma_ref,
-    blocks_ref,
-    out_ref,
-    near_right_ref,
-    near_shuffled_ref,
-    wide_ref,
-    scratch_ref,
-    right_ref,
-    shuffled_ref,
-):
+def density_kernel(order, rows, padded, start_ref, sigma_ref, blocks_ref, out_ref, wide_ref):
     slots, _, slab, width = blocks_ref.shape[1:]
-    padded = right_ref.shape[3] // 2
-    devices = len(orders[0])
+    devices = len(order)
     row = lax.axis_index("rows")
     odd = lax.rem(row, 2)
-    keep = [jnp.where(row == 0, 0.0, 1.0), jnp.where(row == rows - 1, 0.0, 1.0)]
-    sides = [spread_rows(sigma_ref.at[side], wide_ref, slab, padded, orders[side]) for side in range(2)]
+    has_far = jnp.where(jnp.logical_and(row > 0, row < rows - 1), 1.0, 0.0)
+    own = spread_rows(sigma_ref.at[1 - odd], wide_ref.at[0], slab, padded, order)
+    far = spread_rows(sigma_ref.at[odd], wide_ref.at[1], slab, padded, order)
     on_diagonal = row_positions(slab, devices, (slab, padded)) == lax.broadcasted_iota(jnp.int32, (slab, padded), 1)
     diagonal = jnp.concatenate(
-        [
-            jnp.sum(jnp.where(on_diagonal, jnp.where(odd == 1, upper, lower), 0.0), axis=0, keepdims=True)
-            for upper, lower in zip(*sides)
-        ],
-        axis=0,
+        [jnp.sum(jnp.where(on_diagonal, matrix, 0.0), axis=0, keepdims=True) for matrix in own], axis=0
     )
     at_row = lax.broadcasted_iota(jnp.int32, (padded, width), 0)
     placed = at_row + start_ref[0] == lax.broadcasted_iota(jnp.int32, (padded, width), 1)
     place = jnp.where(jnp.logical_and(placed, at_row < slab), 1.0, 0.0).astype(BF16)
     direct = jnp.dot(diagonal.astype(BF16), place, preferred_element_type=F32)
+    ordering = row_order(slab, devices)
     for slot in range(slots):
-        found = []
-        for side in range(2):
-            block = side + odd
-            mine = (right_ref.at[slot, side], shuffled_ref.at[slot, side])
-            prepare_block(
-                blocks_ref[0, slot, block], blocks_ref[1, slot, block], *mine, scratch_ref.at[slot, side], devices
-            )
-            found.append(neighbour_density(sides[side], *mine, slot))
+        here = neighbour_density(own, blocks_ref, slot, 1, ordering)
+        there = neighbour_density(far, blocks_ref, slot, 2 * odd, ordering)
         for kind in range(2):
             for part in range(2):
                 at = slot * 4 + kind * 2 + part
-                both = found[0][kind][part] * keep[0] + found[1][kind][part] * keep[1]
                 out_ref[(kind * 2 + part) * slots + slot] = direct[at : at + 1] + jnp.sum(
-                    both, axis=0, keepdims=True
+                    here[kind][part] + there[kind][part] * has_far, axis=0, keepdims=True
                 )
+
+
+def density_near_kernel(order, padded, sigma_ref, blocks_ref, before_ref, out_ref, wide_ref):
+    slots, _, slab, _ = blocks_ref.shape[1:]
+    near = spread_rows(sigma_ref, wide_ref, slab, padded, order)
+    ordering = row_order(slab, len(order))
+    block = 2 - 2 * lax.rem(lax.axis_index("rows"), 2)
     for slot in range(slots):
-        block = 2 - 2 * odd
-        prepare_block(
-            blocks_ref[0, slot, block],
-            blocks_ref[1, slot, block],
-            near_right_ref.at[slot],
-            near_shuffled_ref.at[slot],
-            scratch_ref.at[slot, 2],
-            devices,
-        )
-
-
-def density_near_kernel(orders, sigma_ref, right_ref, shuffled_ref, before_ref, out_ref, wide_ref):
-    slots, slab, padded = shuffled_ref.shape[0], shuffled_ref.shape[2], right_ref.shape[2] // 2
-    odd = lax.rem(lax.axis_index("rows"), 2)
-    places = [jnp.where(odd == 1, even_row, odd_row) for odd_row, even_row in zip(*orders)]
-    near = spread_rows(sigma_ref, wide_ref, slab, padded, places)
-    for slot in range(slots):
-        found = neighbour_density(near, right_ref.at[slot], shuffled_ref.at[slot], slot)
+        found = neighbour_density(near, blocks_ref, slot, block, ordering)
         for kind in range(2):
             for part in range(2):
                 at = (kind * 2 + part) * slots + slot
@@ -314,14 +259,13 @@
     total = devices * slots
     columns = entries // devices
     order = exchange_order(devices)
-    orders = shuffled_orders(devices)
     padded = pl.cdiv(slab, 128) * 128
 
     def stay(values):
         return pltpu.with_memory_space_constraint(values, pltpu.HBM)
 
     packed, first, second = call(
-        functools.partial(front_kernel, order, orders[0]),
+        functools.partial(front_kernel, order),
         (
             jax.ShapeDtypeStruct((4 * total, columns), BF16),
             jax.ShapeDtypeStruct((4 * total, 2 * 4 * total), BF16),
@@ -341,14 +285,14 @@
         packed, "energy", split_axis=0, concat_axis=0, tiled=True, axis_index_groups=[order]
     )
     sigma = call(
-        functools.partial(convolve_kernel, orders),
+        convolve_kernel,
         jax.ShapeDtypeStruct((2, 4 * total, columns), BF16),
         [VMEM] * 4,
         2 * 5 * 16 * total * total * columns,
     )(first, second, spread, screened.reshape(4 * total, columns))
 
     groups = [
-        [energy * rows + (low + side) % rows for side in range(2) for energy in orders[side]]
+        [energy * rows + (low + side) % rows for side in range(2) for energy in order]
         for low in range(1, rows, 2)
     ]
     both = lax.all_to_all(
@@ -363,28 +307,24 @@
     pairs = [(row, row ^ 1) for row in range(rows)]
     near = lax.ppermute(own, "rows", pairs)
 
-    spreading = pltpu.VMEM((pl.cdiv(columns + padded - slab, 128), 4 * total, 128), F32)
+    blocks = retarded.reshape(2, slots, 3, slab, width)
+    wide = (pl.cdiv(columns + padded - slab, 128), 4 * total, 128)
     out = jax.ShapeDtypeStruct((4 * slots, 1, width), F32)
     work = 2 * 8 * slots * 2 * slab * slab * width
-    density, right, shuffled = call(
-        functools.partial(density_kernel, orders, rows),
-        (
-            out,
-            jax.ShapeDtypeStruct((slots, 2, 2 * padded, width), BF16),
-            jax.ShapeDtypeStruct((slots, 2, slab, width), F32),
-        ),
+    density = call(
+        functools.partial(density_kernel, order, rows, padded),
+        out,
         [SMEM] + [VMEM] * 2,
         2 * work,
-        [
-            spreading,
-            pltpu.VMEM((slots, 3, pl.cdiv(width, 128), slab, 128), F32),
-            pltpu.VMEM((slots, 2, 2, 2 * padded, width), BF16),
-            pltpu.VMEM((slots, 2, 2, slab, width), F32),
-        ],
-    )(window_start, both, retarded.reshape(2, slots, 3, slab, width))
-    density = call(functools.partial(density_near_kernel, orders), out, [VMEM] * 4, work, [spreading])(
-        near, right, shuffled, density
-    )
+        [pltpu.VMEM((2, *wide), F32)],
+    )(window_start, both, blocks)
+    density = call(
+        functools.partial(density_near_kernel, order, padded),
+        out,
+        [VMEM] * 3,
+        work,
+        [pltpu.VMEM(wide, F32)],
+    )(near, blocks, density)
     return density.reshape(2, 2, slots, 1, width)
 
 

time: 29.4 us -> 29.4 us (level)
  transfers between devices with their start and end apart: 1 -> 1, of which waited for: 0 -> 0; matrix products, arithmetic and copies ran while one was open for 0% -> 0% of each run, Pallas kernels for 4% -> 3%
where the time goes in v4:
time: 29.4 us; the launch traced here: 29 us
  blocking collectives  24.6 us (84%)
  Pallas kernels  3.35 us (11%)
  between operations  0.7 us (2%)
  starting transfers between devices  0.39 us (1%)
    all_to_all x1, blocking collectives, shards(): lax.all_to_all(sigma.reshape(2 * devices, 4 * slots, columns), ('energy',...  15.2 us
    all_to_all x1, blocking collectives, shards(): lax.all_to_all(packed, 'energy', split_axis=0, concat_axis=0, tiled=True,...  9.35 us
    pallas_call x1, Pallas kernels, shards(): call(functools.partial(front_kernel, order), (jax.ShapeDtypeStruct((4 * t...  1.06 us
    pallas_call x1, Pallas kernels, shards(): call(functools.partial(density_near_kernel, order, padded), out, [VMEM] *...  1.05 us
    pallas_call x1, Pallas kernels, shards(): call(functools.partial(density_kernel, order, rows, padded), out, [SMEM]...  0.84 us
  transfers between devices with their start and end apart: 1, of which 0 were waited for; matrix products, arithmetic and copies ran while one was open for 0% of the time, Pallas kernels for 3%

profile of v4, /device:TPU:1, one launch (start us, length us, event | category | flops | bytes accessed | tf_op | source)
XLA Modules:
  0.0 29.0 jit_solution(18028559132970024149)
XLA Ops:
  0.0 1.1 %shard_map.55 = (bf16[64,1152]{1,0:T(8,128)(2,1)S(1)}, bf16[64,128]{1,0:T(8,128)(2,1)S(1)}, bf16[64,192]{1,0:T(8,128)(2,1)S(1)}) custom-call(s32[1,16]{1,0:T(1,128)} %bitcast.19, bf16[4,2,9216]{2,1,0:T(2,128)(2,1)} %bitcast.18), custom_call_target="tpu_custom_call" | custom-call | flops 1000 | bytes 1048576 | tf_op jit(solution)/shard_map/pallas_call | solution.py:267
  1.1 0.0 copy-start.1
  1.1 9.4 %all_to_all.16 = bf16[8,8,1152]{2,1,0:T(8,128)(2,1)S(1)} all-to-all(bf16[8,8,1152]{2,1,0:T(8,128)(2,1)S(1)} %bitcast.17), channel_id=1, replica_groups={{20,16,12,8,4,0,28,24},{21,17,13,9,5,1,29,25},{22,18,14,10,6,2,30,26},{..., dimensions={0} | all-to-all | bytes 294912 | tf_op jit(solution)/shard_map/all_to_all | solution.py:284
  10.4 0.0 copy-done.1
  10.4 0.4 %shard_map.56 = bf16[2,64,1152]{2,1,0:T(8,128)(2,1)S(1)} custom-call(bf16[64,128]{1,0:T(8,128)(2,1)S(1)} %get-tuple-element.16.first_ref, bf16[64,192]{1,0:T(8,128)(2,1)S(1)} %get-tuple-element.17.second_ref, bf16[64,1152]{1,0:T(8,128)(2,1)S(1)} %bitcast.15, bf16[64,1152]{1,0:T(8,128)(2,1)S(1)} %bitcast.16), custom_call_target="tpu_custom_call" | custom-call | flops 47185920 | bytes 1048576 | tf_op jit(solution)/shard_map/pallas_call | solution.py:287
  10.8 0.0 copy-start
  10.8 15.2 %all_to_all.17 = bf16[16,8,1152]{2,1,0:T(8,128)(2,1)S(1)} all-to-all(bf16[16,8,1152]{2,1,0:T(8,128)(2,1)S(1)} %bitcast.14), channel_id=1, replica_groups={{21,17,13,9,5,1,29,25,22,18,14,10,6,2,30,26},{23,19,15,11,7,3,31,27,20,..., dimensions={0} | all-to-all | bytes 589824 | tf_op jit(solution)/shard_map/all_to_all | solution.py:298
  26.1 0.4 %collective-permute-start = (bf16[64,1152]{1,0:T(8,128)(2,1)S(1)}, bf16[64,1152]{1,0:T(8,128)(2,1)S(1)}, u32[]{:S(2)}, u32[]{:S(2)}) collective-permute-start(bf16[64,1152]{1,0:T(8,128)(2,1)S(1)} %fusion), channel_id=1, source_target_pairs={{0,1},{1,0},{2,3},{3,2},{4,5},{5,4},{6,7},{7,6},{8,9},{9,8},{10,11... | collective-permute-start | bytes 442376 | tf_op jit(solution)/shard_map/ppermute | solution.py:308
  27.1 0.0 copy-done
  27.1 0.8 %shard_map.57.before_ref = f32[8,1,192]{2,1,0:T(1,128)S(1)} custom-call(s32[1]{0:T(128)S(6)} %copy.6.start_ref, bf16[2,64,1152]{2,1,0:T(8,128)(2,1)S(1)} %bitcast.11, bf16[2,2,3,96,192]{4,3,2,1,0:T(8,128)(2,1)S(1)} %bitcast.12), custom_call_target="tpu_custom_call" | custom-call | flops 226492416 | bytes 1048576 | tf_op jit(solution)/shard_map/pallas_call | solution.py:314
  28.0 0.0 collective-permute-done.sigma_ref
  28.0 1.1 %shard_map.58 = f32[8,1,192]{2,1,0:T(1,128)} custom-call(bf16[64,1152]{1,0:T(8,128)(2,1)S(1)} %collective-permute-done.sigma_ref, bf16[2,2,3,96,192]{4,3,2,1,0:T(8,128)(2,1)S(1)} %bitcast.13, f32[8,1,192]{2,1,0:T(1,128)S(1)} %shard_map.57.before_ref), custom_call_target="tpu_custom_call" | custom-call | flops 113246208 | bytes 1048576 | tf_op jit(solution)/shard_map/pallas_call | solution.py:321
  (1 shorter events, 0.0 us)
Async XLA Ops:
  1.1 9.4 %copy-start.1 = (bf16[2,2,16,1,1152]{4,2,3,1,0:T(8,128)(2,1)S(1)}, bf16[2,2,16,1,1152]{4,2,3,1,0:T(8,128)(2,1)}, u32[]{:S(2)}) copy-start(bf16[2,2,16,1,1152]{4,2,3,1,0:T(8,128)(2,1)} %param.6) | copy-start | bytes 442372
  10.8 16.3 %copy-start = (bf16[2,2,1,3,96,192]{5,4,3,2,1,0:T(8,128)(2,1)S(1)}, bf16[2,2,1,3,96,192]{5,4,3,2,1,0:T(8,128)(2,1)}, u32[]{:S(2)}) copy-start(bf16[2,2,1,3,96,192]{5,4,3,2,1,0:T(8,128)(2,1)} %param.7) | copy-start | bytes 1327108
  26.1 1.9 %collective-permute-start = (bf16[64,1152]{1,0:T(8,128)(2,1)S(1)}, bf16[64,1152]{1,0:T(8,128)(2,1)S(1)}, u32[]{:S(2)}, u32[]{:S(2)}) collective-permute-start(bf16[64,1152]{1,0:T(8,128)(2,1)S(1)} %fusion), channel_id=1, source_target_pairs={{0,1},{1,0},{2,3},{3,2},{4,5},{5,4},{6,7},{7,6},{8,9},{9,8},{10,11... | collective-permute-start | bytes 442376 | tf_op jit(solution)/shard_map/ppermute | solution.py:308

commit v5 on v4

--- a/solution.py
+++ b/solution.py
@@ -134,10 +134,9 @@
     copies[1].wait()
     pairs, slots, entries = green_ref.shape
     columns = entries // len(order)
-    rows = pairs * slots
     whole = jnp.concatenate([green_ref[at].astype(F32) for at in range(pairs)], axis=0)
-    for at, device in enumerate(order):
-        out_ref[at * rows : (at + 1) * rows, :] = whole[:, device * columns : (device + 1) * columns].astype(BF16)
+    parts = [whole[:, device * columns : (device + 1) * columns] for device in order]
+    out_ref[...] = jnp.concatenate(parts, axis=0).astype(BF16)
 
 
 def convolve_kernel(first_ref, second_ref, spread_ref, screen_ref, out_ref):

time: 29.4 us -> 29.4 us (level)
  no operation moved by 1% of the time
where the time goes in v5:
time: 29.4 us; the launch traced here: 29 us
  blocking collectives  24.6 us (84%)
  Pallas kernels  3.35 us (11%)
  between operations  0.7 us (2%)
  starting transfers between devices  0.39 us (1%)
    all_to_all x1, blocking collectives, shards(): lax.all_to_all(sigma.reshape(2 * devices, 4 * slots, columns), ('energy',...  15.2 us
    all_to_all x1, blocking collectives, shards(): lax.all_to_all(packed, 'energy', split_axis=0, concat_axis=0, tiled=True,...  9.35 us
    pallas_call x1, Pallas kernels, shards(): call(functools.partial(front_kernel, order), (jax.ShapeDtypeStruct((4 * t...  1.06 us
    pallas_call x1, Pallas kernels, shards(): call(functools.partial(density_near_kernel, order, padded), out, [VMEM] *...  1.05 us
    pallas_call x1, Pallas kernels, shards(): call(functools.partial(density_kernel, order, rows, padded), out, [SMEM]...  0.84 us
  transfers between devices with their start and end apart: 1, of which 0 were waited for; matrix products, arithmetic and copies ran while one was open for 0% of the time, Pallas kernels for 3%

profile of v5, /device:TPU:1, one launch (start us, length us, event | category | flops | bytes accessed | tf_op | source)
XLA Modules:
  0.0 29.0 jit_solution(18028559132970024149)
XLA Ops:
  0.0 1.1 %shard_map.55 = (bf16[64,1152]{1,0:T(8,128)(2,1)S(1)}, bf16[64,128]{1,0:T(8,128)(2,1)S(1)}, bf16[64,192]{1,0:T(8,128)(2,1)S(1)}) custom-call(s32[1,16]{1,0:T(1,128)} %bitcast.19, bf16[4,2,9216]{2,1,0:T(2,128)(2,1)} %bitcast.18), custom_call_target="tpu_custom_call" | custom-call | flops 1000 | bytes 1048576 | tf_op jit(solution)/shard_map/pallas_call | solution.py:266
  1.1 0.0 copy-start.1
  1.1 9.4 %all_to_all.16 = bf16[8,8,1152]{2,1,0:T(8,128)(2,1)S(1)} all-to-all(bf16[8,8,1152]{2,1,0:T(8,128)(2,1)S(1)} %bitcast.17), channel_id=1, replica_groups={{20,16,12,8,4,0,28,24},{21,17,13,9,5,1,29,25},{22,18,14,10,6,2,30,26},{..., dimensions={0} | all-to-all | bytes 294912 | tf_op jit(solution)/shard_map/all_to_all | solution.py:283
  10.4 0.0 copy-done.1
  10.4 0.4 %shard_map.56 = bf16[2,64,1152]{2,1,0:T(8,128)(2,1)S(1)} custom-call(bf16[64,128]{1,0:T(8,128)(2,1)S(1)} %get-tuple-element.16.first_ref, bf16[64,192]{1,0:T(8,128)(2,1)S(1)} %get-tuple-element.17.second_ref, bf16[64,1152]{1,0:T(8,128)(2,1)S(1)} %bitcast.15, bf16[64,1152]{1,0:T(8,128)(2,1)S(1)} %bitcast.16), custom_call_target="tpu_custom_call" | custom-call | flops 47185920 | bytes 1048576 | tf_op jit(solution)/shard_map/pallas_call | solution.py:286
  10.8 0.0 copy-start
  10.8 15.2 %all_to_all.17 = bf16[16,8,1152]{2,1,0:T(8,128)(2,1)S(1)} all-to-all(bf16[16,8,1152]{2,1,0:T(8,128)(2,1)S(1)} %bitcast.14), channel_id=1, replica_groups={{21,17,13,9,5,1,29,25,22,18,14,10,6,2,30,26},{23,19,15,11,7,3,31,27,20,..., dimensions={0} | all-to-all | bytes 589824 | tf_op jit(solution)/shard_map/all_to_all | solution.py:297
  26.1 0.4 %collective-permute-start = (bf16[64,1152]{1,0:T(8,128)(2,1)S(1)}, bf16[64,1152]{1,0:T(8,128)(2,1)S(1)}, u32[]{:S(2)}, u32[]{:S(2)}) collective-permute-start(bf16[64,1152]{1,0:T(8,128)(2,1)S(1)} %fusion), channel_id=1, source_target_pairs={{0,1},{1,0},{2,3},{3,2},{4,5},{5,4},{6,7},{7,6},{8,9},{9,8},{10,11... | collective-permute-start | bytes 442376 | tf_op jit(solution)/shard_map/ppermute | solution.py:307
  27.1 0.0 copy-done
  27.1 0.8 %shard_map.57.before_ref = f32[8,1,192]{2,1,0:T(1,128)S(1)} custom-call(s32[1]{0:T(128)S(6)} %copy.6.start_ref, bf16[2,64,1152]{2,1,0:T(8,128)(2,1)S(1)} %bitcast.11, bf16[2,2,3,96,192]{4,3,2,1,0:T(8,128)(2,1)S(1)} %bitcast.12), custom_call_target="tpu_custom_call" | custom-call | flops 226492416 | bytes 1048576 | tf_op jit(solution)/shard_map/pallas_call | solution.py:313
  28.0 0.0 collective-permute-done.sigma_ref
  28.0 1.1 %shard_map.58 = f32[8,1,192]{2,1,0:T(1,128)} custom-call(bf16[64,1152]{1,0:T(8,128)(2,1)S(1)} %collective-permute-done.sigma_ref, bf16[2,2,3,96,192]{4,3,2,1,0:T(8,128)(2,1)S(1)} %bitcast.13, f32[8,1,192]{2,1,0:T(1,128)S(1)} %shard_map.57.before_ref), custom_call_target="tpu_custom_call" | custom-call | flops 113246208 | bytes 1048576 | tf_op jit(solution)/shard_map/pallas_call | solution.py:320
  (1 shorter events, 0.0 us)
Async XLA Ops:
  1.1 9.4 %copy-start.1 = (bf16[2,2,16,1,1152]{4,2,3,1,0:T(8,128)(2,1)S(1)}, bf16[2,2,16,1,1152]{4,2,3,1,0:T(8,128)(2,1)}, u32[]{:S(2)}) copy-start(bf16[2,2,16,1,1152]{4,2,3,1,0:T(8,128)(2,1)} %param.6) | copy-start | bytes 442372
  10.8 16.3 %copy-start = (bf16[2,2,1,3,96,192]{5,4,3,2,1,0:T(8,128)(2,1)S(1)}, bf16[2,2,1,3,96,192]{5,4,3,2,1,0:T(8,128)(2,1)}, u32[]{:S(2)}) copy-start(bf16[2,2,1,3,96,192]{5,4,3,2,1,0:T(8,128)(2,1)} %param.7) | copy-start | bytes 1327108
  26.1 1.9 %collective-permute-start = (bf16[64,1152]{1,0:T(8,128)(2,1)S(1)}, bf16[64,1152]{1,0:T(8,128)(2,1)S(1)}, u32[]{:S(2)}, u32[]{:S(2)}) collective-permute-start(bf16[64,1152]{1,0:T(8,128)(2,1)S(1)} %fusion), channel_id=1, source_target_pairs={{0,1},{1,0},{2,3},{3,2},{4,5},{5,4},{6,7},{7,6},{8,9},{9,8},{10,11... | collective-permute-start | bytes 442376 | tf_op jit(solution)/shard_map/ppermute | solution.py:307

commit v6 on v5

--- a/solution.py
+++ b/solution.py
@@ -12,7 +12,6 @@
 BF16 = jnp.bfloat16
 VMEM = pl.BlockSpec(memory_space=pltpu.VMEM)
 SMEM = pl.BlockSpec(memory_space=pltpu.SMEM)
-HBM = pl.BlockSpec(memory_space=pltpu.HBM)
 
 
 def call(kernel, out_shape, in_specs, flops, scratch=(), moved=2**20):
@@ -110,33 +109,20 @@
     return jnp.concatenate(found, axis=1)[:, :lanes]
 
 
-def front_kernel(
-    order,
-    energy_hbm,
-    green_hbm,
-    out_ref,
-    first_ref,
-    second_ref,
-    energy_ref,
-    green_ref,
-    sems,
-):
-    pairs = ((energy_hbm, energy_ref), (green_hbm, green_ref))
-    copies = [pltpu.make_async_copy(source, target, sems.at[at]) for at, (source, target) in enumerate(pairs)]
-    for copy in copies:
-        copy.start()
-    copies[0].wait()
+def pack_kernel(order, green_ref, out_ref):
+    pairs, slots, entries = green_ref.shape
+    columns = entries // len(order)
+    whole = jnp.concatenate([green_ref[at].astype(F32) for at in range(pairs)], axis=0)
+    parts = [whole[:, device * columns : (device + 1) * columns] for device in order]
+    out_ref[...] = jnp.concatenate(parts, axis=0).astype(BF16)
+
+
+def tables_kernel(order, energy_ref, first_ref, second_ref):
     first, second = tables(energy_ref[...], order)
     first_high, first_low = split_high_low(first)
     second_high, second_low = split_high_low(second)
     first_ref[...] = jnp.concatenate([first_high, first_low], axis=1)
     second_ref[...] = jnp.concatenate([second_high, second_low, second_high], axis=1)
-    copies[1].wait()
-    pairs, slots, entries = green_ref.shape
-    columns = entries // len(order)
-    whole = jnp.concatenate([green_ref[at].astype(F32) for at in range(pairs)], axis=0)
-    parts = [whole[:, device * columns : (device + 1) * columns] for device in order]
-    out_ref[...] = jnp.concatenate(parts, axis=0).astype(BF16)
 
 
 def convolve_kernel(first_ref, second_ref, spread_ref, screen_ref, out_ref):
@@ -260,29 +246,23 @@
     order = exchange_order(devices)
     padded = pl.cdiv(slab, 128) * 128
 
-    def stay(values):
-        return pltpu.with_memory_space_constraint(values, pltpu.HBM)
-
-    packed, first, second = call(
-        functools.partial(front_kernel, order),
+    packed = call(
+        functools.partial(pack_kernel, order), jax.ShapeDtypeStruct((4 * total, columns), BF16), [VMEM], 1000
+    )(green_window.reshape(4, slots, entries))
+    first, second = call(
+        functools.partial(tables_kernel, order),
         (
-            jax.ShapeDtypeStruct((4 * total, columns), BF16),
             jax.ShapeDtypeStruct((4 * total, 2 * 4 * total), BF16),
             jax.ShapeDtypeStruct((4 * total, 3 * 4 * total), BF16),
         ),
-        [HBM] * 2,
+        [VMEM],
         1000,
-        [
-            pltpu.VMEM((1, total), jnp.int32),
-            pltpu.VMEM((4, slots, entries), BF16),
-            pltpu.SemaphoreType.DMA((2,)),
-        ],
-    )(stay(energy_order.reshape(1, total)), stay(green_window.reshape(4, slots, entries)))
-    odd = lax.axis_index("rows") % 2 == 1
-    packed, first, second, odd = lax.optimization_barrier((packed, first, second, odd))
+    )(energy_order.reshape(1, total))
     spread = lax.all_to_all(
         packed, "energy", split_axis=0, concat_axis=0, tiled=True, axis_index_groups=[order]
     )
+    odd = lax.axis_index("rows") % 2 == 1
+    spread, first, second, odd = lax.optimization_barrier((spread, first, second, odd))
     sigma = call(
         convolve_kernel,
         jax.ShapeDtypeStruct((2, 4 * total, columns), BF16),

time: 29.4 us -> 31 us (1.054)
  blocking collectives: 24.6 us -> 14.9 us
  starting transfers between devices: 0.39 us -> 7.92 us
  waiting for transfers between devices: 0.01 us -> 2.09 us
  local copies, waits for them, and re-layouts: 0.01 us -> 1.57 us
    all_to_all x1 -> x0, blocking collectives: 9.35 us -> none  [shards(): lax.all_to_all(packed, 'energy', split_axis=0, concat_axis=0, tiled=True,...]
    all_to_all x0 -> x1, starting transfers between devices: none -> 7.53 us  [shards(): lax.all_to_all(packed, 'energy', split_axis=0, concat_axis=0, tiled=True,...]
    all_to_all x0 -> x1, waiting for transfers between devices: none -> 2.09 us  [shards(): lax.all_to_all(packed, 'energy', split_axis=0, concat_axis=0, tiled=True,...]
    unnamed x4 -> x8, local copies, waits for them, and re-layouts: 0.01 us -> 1.57 us
    pallas_call x1 -> x2, Pallas kernels: 1.06 us -> 1.05 us  [the longest x1 0.75 us: shards(): call(functools.partial(pack_kernel, order), jax.ShapeDtypeStruct((4 * tot...]
  transfers between devices with their start and end apart: 1 -> 2, of which waited for: 0 -> 1; matrix products, arithmetic and copies ran while one was open for 0% -> 0% of each run, Pallas kernels for 3% -> 4%
where the time goes in v6:
time: 31 us; the launch traced here: 30.6 us
  blocking collectives  14.9 us (48%)
  starting transfers between devices  7.92 us (26%)
  Pallas kernels  3.34 us (11%)
  waiting for transfers between devices  2.09 us (7%)
  local copies, waits for them, and re-layouts  1.57 us (5%)
  between operations  0.69 us (2%)
    all_to_all x1, blocking collectives, shards(): lax.all_to_all(sigma.reshape(2 * devices, 4 * slots, columns), ('energy',...  14.9 us
    all_to_all x1, starting transfers between devices, shards(): lax.all_to_all(packed, 'energy', split_axis=0, concat_axis=0, tiled=True,...  7.53 us
    all_to_all x1, waiting for transfers between devices, shards(): lax.all_to_all(packed, 'energy', split_axis=0, concat_axis=0, tiled=True,...  2.09 us
    unnamed x8, local copies, waits for them, and re-layouts  1.57 us
    pallas_call x1, Pallas kernels, shards(): call(functools.partial(density_near_kernel, order, padded), out, [VMEM] *...  1.05 us
    pallas_call x1, Pallas kernels, shards(): call(functools.partial(density_kernel, order, rows, padded), out, [SMEM]...  0.84 us
    pallas_call x1, Pallas kernels, shards(): call(functools.partial(pack_kernel, order), jax.ShapeDtypeStruct((4 * tot...  0.75 us
  transfers between devices with their start and end apart: 2, of which 1 were waited for; matrix products, arithmetic and copies ran while one was open for 0% of the time, Pallas kernels for 4%

profile of v6, /device:TPU:1, one launch (start us, length us, event | category | flops | bytes accessed | tf_op | source)
XLA Modules:
  0.0 30.6 jit_solution(4375005485196776134)
XLA Ops:
  0.0 0.0 copy-start.2
  0.0 0.9 %copy-done.2 = bf16[2,2,2,1,9216]{4,2,3,1,0:T(2,128)(2,1)S(1)} copy-done((bf16[2,2,2,1,9216]{4,2,3,1,0:T(2,128)(2,1)S(1)}, bf16[2,2,2,1,9216]{4,2,3,1,0:T(2,128)(2,1)}, u32[]{:S(2)}) %copy-start.2) | copy-done | bytes 147480
  0.9 0.7 %shard_map.55 = bf16[64,1152]{1,0:T(8,128)(2,1)} custom-call(bf16[4,2,9216]{2,1,0:T(2,128)(2,1)S(1)} %bitcast.17), custom_call_target="tpu_custom_call" | custom-call | flops 1000 | bytes 1048576 | tf_op jit(solution)/shard_map/pallas_call | solution.py:249
  1.7 0.0 copy-start.1
  1.7 7.5 %all-to-all-start = ((bf16[8,8,1152]{2,1,0:T(8,128)(2,1)}), bf16[8,8,1152]{2,1,0:T(8,128)(2,1)S(1)}, u32[]{:S(2)}, u32[]{:S(2)}) async-start(bf16[8,8,1152]{2,1,0:T(8,128)(2,1)} %bitcast.1), calls=%async_computation | async-start | bytes 294912 | tf_op jit(solution)/shard_map/all_to_all | solution.py:261
  9.2 0.0 copy-start.3
  9.2 0.7 %copy-done.3 = s32[16]{0:T(128)S(1)} copy-done((s32[16]{0:T(128)S(1)}, s32[16]{0:T(128)}, u32[]{:S(2)}) %copy-start.3) | copy-done | bytes 88
  9.8 0.3 shard_map.56
  10.1 2.1 %all-to-all-done = bf16[8,8,1152]{2,1,0:T(8,128)(2,1)S(1)} async-done(((bf16[8,8,1152]{2,1,0:T(8,128)(2,1)}), bf16[8,8,1152]{2,1,0:T(8,128)(2,1)S(1)}, u32[]{:S(2)}, u32[]{:S(2)}) %all-to-all-start) | async-done | bytes 147488 | tf_op jit(solution)/shard_map/all_to_all | solution.py:261
  12.2 0.0 copy-done.1
  12.2 0.4 %shard_map.57 = bf16[2,64,1152]{2,1,0:T(8,128)(2,1)S(1)} custom-call(bf16[64,128]{1,0:T(8,128)(2,1)S(1)} %get-tuple-element.14.first_ref, bf16[64,192]{1,0:T(8,128)(2,1)S(1)} %get-tuple-element.15.second_ref, bf16[64,1152]{1,0:T(8,128)(2,1)S(1)} %bitcast.15, bf16[64,1152]{1,0:T(8,128)(2,1)S(1)} %bitcast.16), custom_call_target="tpu_custom_call" | custom-call | flops 47185920 | bytes 1048576 | tf_op jit(solution)/shard_map/pallas_call | solution.py:266
  12.6 0.0 copy-start
  12.6 14.9 %all_to_all.17 = bf16[16,8,1152]{2,1,0:T(8,128)(2,1)S(1)} all-to-all(bf16[16,8,1152]{2,1,0:T(8,128)(2,1)S(1)} %bitcast.14), channel_id=1, replica_groups={{21,17,13,9,5,1,29,25,22,18,14,10,6,2,30,26},{23,19,15,11,7,3,31,27,20,..., dimensions={0} | all-to-all | bytes 589824 | tf_op jit(solution)/shard_map/all_to_all | solution.py:277
  27.6 0.4 %collective-permute-start = (bf16[64,1152]{1,0:T(8,128)(2,1)S(1)}, bf16[64,1152]{1,0:T(8,128)(2,1)S(1)}, u32[]{:S(2)}, u32[]{:S(2)}) collective-permute-start(bf16[64,1152]{1,0:T(8,128)(2,1)S(1)} %fusion), channel_id=1, source_target_pairs={{0,1},{1,0},{2,3},{3,2},{4,5},{5,4},{6,7},{7,6},{8,9},{9,8},{10,11... | collective-permute-start | bytes 442376 | tf_op jit(solution)/shard_map/ppermute | solution.py:287
  28.6 0.0 copy-done
  28.6 0.8 %shard_map.58.before_ref = f32[8,1,192]{2,1,0:T(1,128)S(1)} custom-call(s32[1]{0:T(128)S(6)} %copy.6.start_ref, bf16[2,64,1152]{2,1,0:T(8,128)(2,1)S(1)} %bitcast.11, bf16[2,2,3,96,192]{4,3,2,1,0:T(8,128)(2,1)S(1)} %bitcast.12), custom_call_target="tpu_custom_call" | custom-call | flops 226492416 | bytes 1048576 | tf_op jit(solution)/shard_map/pallas_call | solution.py:293
  29.5 0.0 collective-permute-done.sigma_ref
  29.5 1.1 %shard_map.59 = f32[8,1,192]{2,1,0:T(1,128)} custom-call(bf16[64,1152]{1,0:T(8,128)(2,1)S(1)} %collective-permute-done.sigma_ref, bf16[2,2,3,96,192]{4,3,2,1,0:T(8,128)(2,1)S(1)} %bitcast.13, f32[8,1,192]{2,1,0:T(1,128)S(1)} %shard_map.58.before_ref), custom_call_target="tpu_custom_call" | custom-call | flops 113246208 | bytes 1048576 | tf_op jit(solution)/shard_map/pallas_call | solution.py:300
  (1 shorter events, 0.0 us)
Async XLA Ops:
  0.0 0.9 %copy-start.2 = (bf16[2,2,2,1,9216]{4,2,3,1,0:T(2,128)(2,1)S(1)}, bf16[2,2,2,1,9216]{4,2,3,1,0:T(2,128)(2,1)}, u32[]{:S(2)}) copy-start(bf16[2,2,2,1,9216]{4,2,3,1,0:T(2,128)(2,1)} %param.5) | copy-start | bytes 442372
  1.7 10.6 %copy-start.1 = (bf16[2,2,16,1,1152]{4,2,3,1,0:T(8,128)(2,1)S(1)}, bf16[2,2,16,1,1152]{4,2,3,1,0:T(8,128)(2,1)}, u32[]{:S(2)}) copy-start(bf16[2,2,16,1,1152]{4,2,3,1,0:T(8,128)(2,1)} %param.6) | copy-start | bytes 442372
  1.7 10.6 %all-to-all-start = ((bf16[8,8,1152]{2,1,0:T(8,128)(2,1)}), bf16[8,8,1152]{2,1,0:T(8,128)(2,1)S(1)}, u32[]{:S(2)}, u32[]{:S(2)}) async-start(bf16[8,8,1152]{2,1,0:T(8,128)(2,1)} %bitcast.1), calls=%async_computation | async-start | bytes 294912 | tf_op jit(solution)/shard_map/all_to_all | solution.py:261
  9.2 0.7 %copy-start.3 = (s32[16]{0:T(128)S(1)}, s32[16]{0:T(128)}, u32[]{:S(2)}) copy-start(s32[16]{0:T(128)} %param.8) | copy-start | bytes 196
  12.6 16.0 %copy-start = (bf16[2,2,1,3,96,192]{5,4,3,2,1,0:T(8,128)(2,1)S(1)}, bf16[2,2,1,3,96,192]{5,4,3,2,1,0:T(8,128)(2,1)}, u32[]{:S(2)}) copy-start(bf16[2,2,1,3,96,192]{5,4,3,2,1,0:T(8,128)(2,1)} %param.7) | copy-start | bytes 1327108
  27.6 1.9 %collective-permute-start = (bf16[64,1152]{1,0:T(8,128)(2,1)S(1)}, bf16[64,1152]{1,0:T(8,128)(2,1)S(1)}, u32[]{:S(2)}, u32[]{:S(2)}) collective-permute-start(bf16[64,1152]{1,0:T(8,128)(2,1)S(1)} %fusion), channel_id=1, source_target_pairs={{0,1},{1,0},{2,3},{3,2},{4,5},{5,4},{6,7},{7,6},{8,9},{9,8},{10,11... | collective-permute-start | bytes 442376 | tf_op jit(solution)/shard_map/ppermute | solution.py:287

commit v7 on v5

--- a/solution.py
+++ b/solution.py
@@ -29,7 +29,8 @@
 
 def exchange_order(count):
     middle = count // 2 + 1
-    return [(middle - at) % count for at in range(count)]
+    step = 3 if math.gcd(3, count) == 1 else 1
+    return [(middle + step * at) % count for at in range(count)]
 
 
 def split_high_low(values):

time: 29.4 us -> 29.2 us (level)
    all_to_all x1, blocking collectives: 15.2 us -> 14.9 us  [shards(): lax.all_to_all(sigma.reshape(2 * devices, 4 * slots, columns), ('energy',...]
where the time goes in v7:
time: 29.2 us; the launch traced here: 28.8 us
  blocking collectives  24.4 us (84%)
  Pallas kernels  3.34 us (11%)
  between operations  0.7 us (2%)
  starting transfers between devices  0.39 us (1%)
    all_to_all x1, blocking collectives, shards(): lax.all_to_all(sigma.reshape(2 * devices, 4 * slots, columns), ('energy',...  14.9 us
    all_to_all x1, blocking collectives, shards(): lax.all_to_all(packed, 'energy', split_axis=0, concat_axis=0, tiled=True,...  9.45 us
    pallas_call x1, Pallas kernels, shards(): call(functools.partial(front_kernel, order), (jax.ShapeDtypeStruct((4 * t...  1.06 us
    pallas_call x1, Pallas kernels, shards(): call(functools.partial(density_near_kernel, order, padded), out, [VMEM] *...  1.05 us
    pallas_call x1, Pallas kernels, shards(): call(functools.partial(density_kernel, order, rows, padded), out, [SMEM]...  0.83 us
  transfers between devices with their start and end apart: 1, of which 0 were waited for; matrix products, arithmetic and copies ran while one was open for 0% of the time, Pallas kernels for 3%

profile of v7, /device:TPU:1, one launch (start us, length us, event | category | flops | bytes accessed | tf_op | source)
XLA Modules:
  0.0 28.8 jit_solution(3001309417541299639)
XLA Ops:
  0.0 1.1 %shard_map.55 = (bf16[64,1152]{1,0:T(8,128)(2,1)S(1)}, bf16[64,128]{1,0:T(8,128)(2,1)S(1)}, bf16[64,192]{1,0:T(8,128)(2,1)S(1)}) custom-call(s32[1,16]{1,0:T(1,128)} %bitcast.19, bf16[4,2,9216]{2,1,0:T(2,128)(2,1)} %bitcast.18), custom_call_target="tpu_custom_call" | custom-call | flops 1000 | bytes 1048576 | tf_op jit(solution)/shard_map/pallas_call | solution.py:267
  1.1 0.0 copy-start.1
  1.1 9.5 %all_to_all.16 = bf16[8,8,1152]{2,1,0:T(8,128)(2,1)S(1)} all-to-all(bf16[8,8,1152]{2,1,0:T(8,128)(2,1)S(1)} %bitcast.17), channel_id=1, replica_groups={{20,0,12,24,4,16,28,8},{21,1,13,25,5,17,29,9},{22,2,14,26,6,18,30,10},{..., dimensions={0} | all-to-all | bytes 294912 | tf_op jit(solution)/shard_map/all_to_all | solution.py:284
  10.5 0.0 copy-done.1
  10.5 0.4 %shard_map.56 = bf16[2,64,1152]{2,1,0:T(8,128)(2,1)S(1)} custom-call(bf16[64,128]{1,0:T(8,128)(2,1)S(1)} %get-tuple-element.16.first_ref, bf16[64,192]{1,0:T(8,128)(2,1)S(1)} %get-tuple-element.17.second_ref, bf16[64,1152]{1,0:T(8,128)(2,1)S(1)} %bitcast.15, bf16[64,1152]{1,0:T(8,128)(2,1)S(1)} %bitcast.16), custom_call_target="tpu_custom_call" | custom-call | flops 47185920 | bytes 1048576 | tf_op jit(solution)/shard_map/pallas_call | solution.py:287
  10.9 0.0 copy-start
  10.9 14.9 %all_to_all.17 = bf16[16,8,1152]{2,1,0:T(8,128)(2,1)S(1)} all-to-all(bf16[16,8,1152]{2,1,0:T(8,128)(2,1)S(1)} %bitcast.14), channel_id=1, replica_groups={{21,1,13,25,5,17,29,9,22,2,14,26,6,18,30,10},{23,3,15,27,7,19,31,11,20,..., dimensions={0} | all-to-all | bytes 589824 | tf_op jit(solution)/shard_map/all_to_all | solution.py:298
  25.9 0.4 %collective-permute-start = (bf16[64,1152]{1,0:T(8,128)(2,1)S(1)}, bf16[64,1152]{1,0:T(8,128)(2,1)S(1)}, u32[]{:S(2)}, u32[]{:S(2)}) collective-permute-start(bf16[64,1152]{1,0:T(8,128)(2,1)S(1)} %fusion), channel_id=1, source_target_pairs={{0,1},{1,0},{2,3},{3,2},{4,5},{5,4},{6,7},{7,6},{8,9},{9,8},{10,11... | collective-permute-start | bytes 442376 | tf_op jit(solution)/shard_map/ppermute | solution.py:308
  26.9 0.0 copy-done
  26.9 0.8 %shard_map.57.before_ref = f32[8,1,192]{2,1,0:T(1,128)S(1)} custom-call(s32[1]{0:T(128)S(6)} %copy.6.start_ref, bf16[2,64,1152]{2,1,0:T(8,128)(2,1)S(1)} %bitcast.11, bf16[2,2,3,96,192]{4,3,2,1,0:T(8,128)(2,1)S(1)} %bitcast.12), custom_call_target="tpu_custom_call" | custom-call | flops 226492416 | bytes 1048576 | tf_op jit(solution)/shard_map/pallas_call | solution.py:314
  27.8 0.0 collective-permute-done.sigma_ref
  27.8 1.1 %shard_map.58 = f32[8,1,192]{2,1,0:T(1,128)} custom-call(bf16[64,1152]{1,0:T(8,128)(2,1)S(1)} %collective-permute-done.sigma_ref, bf16[2,2,3,96,192]{4,3,2,1,0:T(8,128)(2,1)S(1)} %bitcast.13, f32[8,1,192]{2,1,0:T(1,128)S(1)} %shard_map.57.before_ref), custom_call_target="tpu_custom_call" | custom-call | flops 113246208 | bytes 1048576 | tf_op jit(solution)/shard_map/pallas_call | solution.py:321
  (1 shorter events, 0.0 us)
Async XLA Ops:
  1.1 9.5 %copy-start.1 = (bf16[2,2,16,1,1152]{4,2,3,1,0:T(8,128)(2,1)S(1)}, bf16[2,2,16,1,1152]{4,2,3,1,0:T(8,128)(2,1)}, u32[]{:S(2)}) copy-start(bf16[2,2,16,1,1152]{4,2,3,1,0:T(8,128)(2,1)} %param.6) | copy-start | bytes 442372
  10.9 16.0 %copy-start = (bf16[2,2,1,3,96,192]{5,4,3,2,1,0:T(8,128)(2,1)S(1)}, bf16[2,2,1,3,96,192]{5,4,3,2,1,0:T(8,128)(2,1)}, u32[]{:S(2)}) copy-start(bf16[2,2,1,3,96,192]{5,4,3,2,1,0:T(8,128)(2,1)} %param.7) | copy-start | bytes 1327108
  25.9 1.9 %collective-permute-start = (bf16[64,1152]{1,0:T(8,128)(2,1)S(1)}, bf16[64,1152]{1,0:T(8,128)(2,1)S(1)}, u32[]{:S(2)}, u32[]{:S(2)}) collective-permute-start(bf16[64,1152]{1,0:T(8,128)(2,1)S(1)} %fusion), channel_id=1, source_target_pairs={{0,1},{1,0},{2,3},{3,2},{4,5},{5,4},{6,7},{7,6},{8,9},{9,8},{10,11... | collective-permute-start | bytes 442376 | tf_op jit(solution)/shard_map/ppermute | solution.py:308

commit v8 on v7

--- a/solution.py
+++ b/solution.py
@@ -60,38 +60,47 @@
     return jnp.where(turns >= 2 * count, -value, value)
 
 
-def tables(energy_order, order):
-    total = energy_order.shape[1]
+def table_plan(total, order):
     slots = total // len(order)
     size = 4 * total
     row = lax.broadcasted_iota(jnp.int32, (size, 1), 0)
     col = lax.broadcasted_iota(jnp.int32, (1, size), 1)
 
-    def device_at(place, places):
+    def device_at(place):
         found = jnp.zeros_like(place)
-        for at, device in enumerate(places):
+        for at, device in enumerate(order):
             found = jnp.where(place == at, device, found)
         return found
 
-    across = lax.broadcasted_iota(jnp.int32, (total, total), 1)
-    down = lax.broadcasted_iota(jnp.int32, (total, total), 0)
-    energy_down = jnp.sum(jnp.where(across == down, energy_order, 0), axis=1, keepdims=True)
-
-    source = device_at(parts_of(col, 4 * slots), order) * slots + wrap(col, slots)
-    energy = jnp.sum(
-        jnp.where(lax.broadcasted_iota(jnp.int32, (total, size), 0) == source, energy_down, 0), axis=0, keepdims=True
-    )
-    same = parts_of(row, 2 * total) == wrap(parts_of(col, 2 * slots), 2)
-    quarter = wrap(parts_of(row, total), 2) - wrap(parts_of(col, slots), 2)
-    first = jnp.where(same, phases(energy, wrap(row, total), quarter, total), 0.0)
-    source = device_at(parts_of(row, 4 * slots), order) * slots + wrap(parts_of(row, 4), slots)
-    energy = jnp.sum(
-        jnp.where(lax.broadcasted_iota(jnp.int32, (size, total), 1) == source, energy_order, 0), axis=1, keepdims=True
-    )
-    same = wrap(parts_of(row, 2), 2) == parts_of(col, 2 * total)
-    quarter = 1 - wrap(row, 2) + wrap(parts_of(col, total), 2)
-    second = jnp.where(same, phases(energy, wrap(col, total), quarter, total), 0.0) * (1.0 / total)
-    return first, second
+    same = lax.broadcasted_iota(jnp.int32, (total, total), 0) == lax.broadcasted_iota(jnp.int32, (total, total), 1)
+    source = device_at(parts_of(col, 4 * slots)) * slots + wrap(col, slots)
+    first = (
+        lax.broadcasted_iota(jnp.int32, (total, size), 0) == source,
+        wrap(row, total),
+        wrap(parts_of(row, total), 2) - wrap(parts_of(col, slots), 2),
+        parts_of(row, 2 * total) == wrap(parts_of(col, 2 * slots), 2),
+    )
+    source = device_at(parts_of(row, 4 * slots)) * slots + wrap(parts_of(row, 4), slots)
+    second = (
+        lax.broadcasted_iota(jnp.int32, (size, total), 1) == source,
+        wrap(col, total),
+        1 - wrap(row, 2) + wrap(parts_of(col, total), 2),
+        wrap(parts_of(row, 2), 2) == parts_of(col, 2 * total),
+    )
+    return same, first, second
+
+
+def tables(energy_order, plan):
+    total = energy_order.shape[1]
+    same, first, second = plan
+    down = jnp.sum(jnp.where(same, energy_order, 0), axis=1, keepdims=True)
+    pick, time, quarter, keep = first
+    energy = jnp.sum(jnp.where(pick, down, 0), axis=0, keepdims=True)
+    there = jnp.where(keep, phases(energy, time, quarter, total), 0.0)
+    pick, time, quarter, keep = second
+    energy = jnp.sum(jnp.where(pick, energy_order, 0), axis=1, keepdims=True)
+    back = jnp.where(keep, phases(energy, time, quarter, total), 0.0) * (1.0 / total)
+    return there, back
 
 
 def row_positions(slab, devices, shape):
@@ -122,18 +131,20 @@
     green_ref,
     sems,
 ):
-    pairs = ((energy_hbm, energy_ref), (green_hbm, green_ref))
-    copies = [pltpu.make_async_copy(source, target, sems.at[at]) for at, (source, target) in enumerate(pairs)]
+    pairs, slots, entries = green_ref.shape
+    copies = [pltpu.make_async_copy(energy_hbm, energy_ref, sems.at[pairs])]
+    copies += [pltpu.make_async_copy(green_hbm.at[at], green_ref.at[at], sems.at[at]) for at in range(pairs)]
     for copy in copies:
         copy.start()
+    plan = table_plan(energy_ref.shape[1], order)
     copies[0].wait()
-    first, second = tables(energy_ref[...], order)
+    first, second = tables(energy_ref[...], plan)
     first_high, first_low = split_high_low(first)
     second_high, second_low = split_high_low(second)
     first_ref[...] = jnp.concatenate([first_high, first_low], axis=1)
     second_ref[...] = jnp.concatenate([second_high, second_low, second_high], axis=1)
-    copies[1].wait()
-    pairs, slots, entries = green_ref.shape
+    for copy in copies[1:]:
+        copy.wait()
     columns = entries // len(order)
     whole = jnp.concatenate([green_ref[at].astype(F32) for at in range(pairs)], axis=0)
     parts = [whole[:, device * columns : (device + 1) * columns] for device in order]
@@ -276,7 +287,7 @@
         [
             pltpu.VMEM((1, total), jnp.int32),
             pltpu.VMEM((4, slots, entries), BF16),
-            pltpu.SemaphoreType.DMA((2,)),
+            pltpu.SemaphoreType.DMA((5,)),
         ],
     )(stay(energy_order.reshape(1, total)), stay(green_window.reshape(4, slots, entries)))
     odd = lax.axis_index("rows") % 2 == 1

time: 29.2 us -> 29.3 us (level)
  no operation moved by 1% of the time
where the time goes in v8:
time: 29.3 us; the launch traced here: 28.9 us
  blocking collectives  24.4 us (83%)
  Pallas kernels  3.37 us (12%)
  between operations  0.7 us (2%)
  starting transfers between devices  0.39 us (1%)
    all_to_all x1, blocking collectives, shards(): lax.all_to_all(sigma.reshape(2 * devices, 4 * slots, columns), ('energy',...  14.9 us
    all_to_all x1, blocking collectives, shards(): lax.all_to_all(packed, 'energy', split_axis=0, concat_axis=0, tiled=True,...  9.45 us
    pallas_call x1, Pallas kernels, shards(): call(functools.partial(front_kernel, order), (jax.ShapeDtypeStruct((4 * t...  1.09 us
    pallas_call x1, Pallas kernels, shards(): call(functools.partial(density_near_kernel, order, padded), out, [VMEM] *...  1.05 us
    pallas_call x1, Pallas kernels, shards(): call(functools.partial(density_kernel, order, rows, padded), out, [SMEM]...  0.83 us
  transfers between devices with their start and end apart: 1, of which 0 were waited for; matrix products, arithmetic and copies ran while one was open for 0% of the time, Pallas kernels for 3%

profile of v8, /device:TPU:1, one launch (start us, length us, event | category | flops | bytes accessed | tf_op | source)
XLA Modules:
  0.0 28.9 jit_solution(11213380049984105235)
XLA Ops:
  0.0 1.1 %shard_map.55 = (bf16[64,1152]{1,0:T(8,128)(2,1)S(1)}, bf16[64,128]{1,0:T(8,128)(2,1)S(1)}, bf16[64,192]{1,0:T(8,128)(2,1)S(1)}) custom-call(s32[1,16]{1,0:T(1,128)} %bitcast.19, bf16[4,2,9216]{2,1,0:T(2,128)(2,1)} %bitcast.18), custom_call_target="tpu_custom_call" | custom-call | flops 1000 | bytes 1048576 | tf_op jit(solution)/shard_map/pallas_call | solution.py:278
  1.1 0.0 copy-start.1
  1.1 9.5 %all_to_all.16 = bf16[8,8,1152]{2,1,0:T(8,128)(2,1)S(1)} all-to-all(bf16[8,8,1152]{2,1,0:T(8,128)(2,1)S(1)} %bitcast.17), channel_id=1, replica_groups={{20,0,12,24,4,16,28,8},{21,1,13,25,5,17,29,9},{22,2,14,26,6,18,30,10},{..., dimensions={0} | all-to-all | bytes 294912 | tf_op jit(solution)/shard_map/all_to_all | solution.py:295
  10.6 0.0 copy-done.1
  10.6 0.4 %shard_map.56 = bf16[2,64,1152]{2,1,0:T(8,128)(2,1)S(1)} custom-call(bf16[64,128]{1,0:T(8,128)(2,1)S(1)} %get-tuple-element.16.first_ref, bf16[64,192]{1,0:T(8,128)(2,1)S(1)} %get-tuple-element.17.second_ref, bf16[64,1152]{1,0:T(8,128)(2,1)S(1)} %bitcast.15, bf16[64,1152]{1,0:T(8,128)(2,1)S(1)} %bitcast.16), custom_call_target="tpu_custom_call" | custom-call | flops 47185920 | bytes 1048576 | tf_op jit(solution)/shard_map/pallas_call | solution.py:298
  11.0 0.0 copy-start
  11.0 14.9 %all_to_all.17 = bf16[16,8,1152]{2,1,0:T(8,128)(2,1)S(1)} all-to-all(bf16[16,8,1152]{2,1,0:T(8,128)(2,1)S(1)} %bitcast.14), channel_id=1, replica_groups={{21,1,13,25,5,17,29,9,22,2,14,26,6,18,30,10},{23,3,15,27,7,19,31,11,20,..., dimensions={0} | all-to-all | bytes 589824 | tf_op jit(solution)/shard_map/all_to_all | solution.py:309
  25.9 0.4 %collective-permute-start = (bf16[64,1152]{1,0:T(8,128)(2,1)S(1)}, bf16[64,1152]{1,0:T(8,128)(2,1)S(1)}, u32[]{:S(2)}, u32[]{:S(2)}) collective-permute-start(bf16[64,1152]{1,0:T(8,128)(2,1)S(1)} %fusion), channel_id=1, source_target_pairs={{0,1},{1,0},{2,3},{3,2},{4,5},{5,4},{6,7},{7,6},{8,9},{9,8},{10,11... | collective-permute-start | bytes 442376 | tf_op jit(solution)/shard_map/ppermute | solution.py:319
  27.0 0.0 copy-done
  27.0 0.8 %shard_map.57.before_ref = f32[8,1,192]{2,1,0:T(1,128)S(1)} custom-call(s32[1]{0:T(128)S(6)} %copy.6.start_ref, bf16[2,64,1152]{2,1,0:T(8,128)(2,1)S(1)} %bitcast.11, bf16[2,2,3,96,192]{4,3,2,1,0:T(8,128)(2,1)S(1)} %bitcast.12), custom_call_target="tpu_custom_call" | custom-call | flops 226492416 | bytes 1048576 | tf_op jit(solution)/shard_map/pallas_call | solution.py:325
  27.8 0.0 collective-permute-done.sigma_ref
  27.8 1.1 %shard_map.58 = f32[8,1,192]{2,1,0:T(1,128)} custom-call(bf16[64,1152]{1,0:T(8,128)(2,1)S(1)} %collective-permute-done.sigma_ref, bf16[2,2,3,96,192]{4,3,2,1,0:T(8,128)(2,1)S(1)} %bitcast.13, f32[8,1,192]{2,1,0:T(1,128)S(1)} %shard_map.57.before_ref), custom_call_target="tpu_custom_call" | custom-call | flops 113246208 | bytes 1048576 | tf_op jit(solution)/shard_map/pallas_call | solution.py:332
  (1 shorter events, 0.0 us)
Async XLA Ops:
  1.1 9.5 %copy-start.1 = (bf16[2,2,16,1,1152]{4,2,3,1,0:T(8,128)(2,1)S(1)}, bf16[2,2,16,1,1152]{4,2,3,1,0:T(8,128)(2,1)}, u32[]{:S(2)}) copy-start(bf16[2,2,16,1,1152]{4,2,3,1,0:T(8,128)(2,1)} %param.6) | copy-start | bytes 442372
  11.0 16.0 %copy-start = (bf16[2,2,1,3,96,192]{5,4,3,2,1,0:T(8,128)(2,1)S(1)}, bf16[2,2,1,3,96,192]{5,4,3,2,1,0:T(8,128)(2,1)}, u32[]{:S(2)}) copy-start(bf16[2,2,1,3,96,192]{5,4,3,2,1,0:T(8,128)(2,1)} %param.7) | copy-start | bytes 1327108
  25.9 1.9 %collective-permute-start = (bf16[64,1152]{1,0:T(8,128)(2,1)S(1)}, bf16[64,1152]{1,0:T(8,128)(2,1)S(1)}, u32[]{:S(2)}, u32[]{:S(2)}) collective-permute-start(bf16[64,1152]{1,0:T(8,128)(2,1)S(1)} %fusion), channel_id=1, source_target_pairs={{0,1},{1,0},{2,3},{3,2},{4,5},{5,4},{6,7},{7,6},{8,9},{9,8},{10,11... | collective-permute-start | bytes 442376 | tf_op jit(solution)/shard_map/ppermute | solution.py:319
